TPU v7x, 256 devices: a whole 4x4x8 slice. The times are simulated.
256 devices in a mesh: slot: 16 (over y, x), row: 16 (over z, core).
Axes of the slice: x: 4, y: 4, z: 8, core: 2. Of those that a mesh axis runs over, the one named last changes fastest.
Arguments:
- innovation: bfloat16 [16, 3, 1408, 1408], P('slot', None, 'row'), may hold values from -6 to 6
- clear_mask: int32 [16, 3, 1408, 1408], P('slot', None, 'row'), may hold values 0 or 1
- lag_list: int32 [4], replicated, may hold values from 0 to 15, as said below
Outputs:
- cross_spectra: float32 [2, 4, 3, 1408, 1408], P(None, None, None, 'slot', 'row')
Inputs may be any that keep to these rules, and one draw needn't show every extreme that they name: `lag_list`: both 0 and 15 appear in every list; entries may repeat.
All inputs are finite; a program needn't handle non-finite values. No bound on the sum of `clear_mask` on one device may be relied on, other than what follows from the above.
Results may differ from a plain program's by a relative error of at most 0.009.
Values may be sent and summed in bfloat16 or wider, within the bound.
No kernel may reach another device: no remote copies, remote signals or barrier semaphores. Data moves between devices by JAX's collectives and lax.ppermute only.
A program may use at most 128 MiB of HBM per device.

v0:
```python
import math

import jax
import jax.numpy as jnp
from jax import lax
from jax.sharding import PartitionSpec as P


def from_behind(value, axis, steps):
    count = lax.axis_size(axis)
    first, last = (max(0, -steps), min(count, count - steps))
    return lax.ppermute(value, axis, [(source, source + steps) for source in range(first, last)])


def tables(length):
    indices = jnp.arange(length, dtype=jnp.int32)
    phases = indices[:, None] * indices[None, :] % length
    angles = phases.astype(jnp.float32) * (2.0 * math.pi / length)
    norm_scale = 1.0 / math.sqrt(length)
    return (
        (jnp.cos(angles) * norm_scale).astype(jnp.bfloat16),
        (jnp.sin(angles) * norm_scale).astype(jnp.bfloat16),
    )


def cross_term(earlier, later):
    early_wide = earlier.astype(jnp.float32)
    late_wide = later.astype(jnp.float32)
    pair_real = (early_wide[0] * late_wide[0] + early_wide[1] * late_wide[1]).astype(jnp.bfloat16)
    pair_imag = (early_wide[1] * late_wide[0] - early_wide[0] * late_wide[1]).astype(jnp.bfloat16)
    return jnp.stack([pair_real, pair_imag])


def on_device(innovation, clear_mask, lag_list):
    masked = innovation[0] * clear_mask[0].astype(jnp.bfloat16)
    rows_here = masked.shape[1]
    col_count = masked.shape[2]
    cosine_cols, sine_cols = tables(col_count)
    cosine_rows, sine_rows = tables(rows_here * lax.axis_size("row"))
    pieces = []
    for channel in range(masked.shape[0]):
        channel_block = masked[channel : channel + 1]
        flattened = channel_block.reshape(-1, col_count)
        g_real = jnp.dot(flattened, cosine_cols, preferred_element_type=jnp.float32).astype(
            jnp.bfloat16
        )
        g_imag = (-jnp.dot(flattened, sine_cols, preferred_element_type=jnp.float32)).astype(
            jnp.bfloat16
        )
        channel_block = jnp.stack([g_real, g_imag]).reshape(
            2, channel_block.shape[0], rows_here, col_count
        )
        gathered = lax.all_to_all(channel_block, "row", split_axis=3, concat_axis=2, tiled=True)
        real_part = gathered[0]
        imag_part = gathered[1]
        f_real = jnp.einsum(
            "kr,crq->ckq", cosine_rows, real_part, preferred_element_type=jnp.float32
        ) + jnp.einsum("kr,crq->ckq", sine_rows, imag_part, preferred_element_type=jnp.float32)
        f_imag = jnp.einsum(
            "kr,crq->ckq", cosine_rows, imag_part, preferred_element_type=jnp.float32
        ) - jnp.einsum("kr,crq->ckq", sine_rows, real_part, preferred_element_type=jnp.float32)
        pieces.append(jnp.stack([f_real, f_imag]).astype(jnp.bfloat16))
    spectra = jnp.concatenate(pieces, axis=1)
    slot_count = lax.axis_size("slot")
    counts = (slot_count - lag_list).astype(jnp.float32)
    products = [cross_term(spectra, spectra)]
    passed = spectra
    for distance in range(1, slot_count):
        passed = from_behind(passed, "slot", 1)
        products.append(cross_term(passed, spectra))
    stacked = jnp.stack(products)
    selector = (lag_list[:, None] == jnp.arange(slot_count, dtype=jnp.int32)[None, :]).astype(
        jnp.bfloat16
    )
    partial_value = jnp.einsum(
        "lk,kxcrq->xlcrq", selector, stacked, preferred_element_type=jnp.float32
    )
    summed = lax.psum_scatter(
        partial_value.astype(jnp.bfloat16), "slot", scatter_dimension=3, tiled=True
    ).astype(jnp.float32)
    return summed / counts[None, :, None, None, None]


def solution(mesh):
    placed = (P("slot", None, "row", None), P("slot", None, "row", None), P())
    return jax.shard_map(
        on_device,
        mesh=mesh,
        in_specs=placed,
        out_specs=P(None, None, None, "slot", "row"),
        check_vma=False,
    )
```

profile of v0, /device:TPU:1, one launch (start us, length us, event | category | flops | bytes accessed | tf_op | source)
XLA Modules:
  0.0 1333.2 jit_solution(17784239495038259846)
XLA Ops:
  8.3 32.5 %fusion.57 = bf16[1,88,1408]{2,1,0:T(8,128)(2,1)S(1)} fusion(bf16[1,3,88,1408]{3,2,1,0:T(8,128)(2,1)S(1)} %convert_multiply_fusion), kind=kOutput, calls=%fused_computation.57 | convolution fusion | flops 370968576 | bytes 495616 | tf_op jit(solution)/shard_map/dot_general | solution.py:47
  40.7 32.2 %fusion.52 = bf16[1,88,1408]{2,1,0:T(8,128)(2,1)S(1)} fusion(bf16[1,3,88,1408]{3,2,1,0:T(8,128)(2,1)S(1)} %convert_multiply_fusion), kind=kOutput, calls=%fused_computation.52 | convolution fusion | flops 370844672 | bytes 495616 | tf_op jit(solution)/shard_map/dot_general | solution.py:44
  85.3 32.2 %fusion.53 = bf16[1,88,1408]{2,1,0:T(8,128)(2,1)S(1)} fusion(bf16[1,3,88,1408]{3,2,1,0:T(8,128)(2,1)S(1)} %convert_multiply_fusion), kind=kOutput, calls=%fused_computation.53 | convolution fusion | flops 370844672 | bytes 495616 | tf_op jit(solution)/shard_map/dot_general | solution.py:44
  117.5 32.5 %fusion.56 = bf16[1,88,1408]{2,1,0:T(8,128)(2,1)S(1)} fusion(bf16[1,3,88,1408]{3,2,1,0:T(8,128)(2,1)S(1)} %convert_multiply_fusion), kind=kOutput, calls=%fused_computation.56 | convolution fusion | flops 370968576 | bytes 495616 | tf_op jit(solution)/shard_map/dot_general | solution.py:47
  159.8 32.2 %fusion.54 = bf16[1,88,1408]{2,1,0:T(8,128)(2,1)S(1)} fusion(bf16[1,3,88,1408]{3,2,1,0:T(8,128)(2,1)S(1)} %convert_multiply_fusion), kind=kOutput, calls=%fused_computation.54 | convolution fusion | flops 370844672 | bytes 495616 | tf_op jit(solution)/shard_map/dot_general | solution.py:44
  192.0 32.5 %fusion.55 = bf16[1,88,1408]{2,1,0:T(8,128)(2,1)S(1)} fusion(bf16[1,3,88,1408]{3,2,1,0:T(8,128)(2,1)S(1)} %convert_multiply_fusion), kind=kOutput, calls=%fused_computation.55 | convolution fusion | flops 370968576 | bytes 495616 | tf_op jit(solution)/shard_map/dot_general | solution.py:47
  256.3 32.2 %fusion.16 = f32[88,1408]{1,0:T(8,128)S(1)} fusion(bf16[1408,88]{0,1:T(8,128)(2,1)S(1)} %reshape.221), kind=kOutput, calls=%fused_computation.16 | convolution fusion | flops 370720768 | bytes 743424 | tf_op jit(solution)/shard_map/kr,crq->ckq/dot_general | solution.py:59
  288.5 32.1 %fusion.17 = f32[88,1408]{1,0:T(8,128)S(1)} fusion(bf16[1408,88]{0,1:T(8,128)(2,1)S(1)} %reshape.220), kind=kOutput, calls=%fused_computation.17 | convolution fusion | flops 370720768 | bytes 743424 | tf_op jit(solution)/shard_map/kr,crq->ckq/dot_general | solution.py:56
  320.6 32.3 %fusion.61 = bf16[1,1,1408,88]{2,3,1,0:T(8,128)(2,1)S(1)} fusion(f32[88,1408]{1,0:T(8,128)S(1)} %fusion.16, bf16[1408,88]{0,1:T(8,128)(2,1)S(1)} %reshape.220), kind=kOutput, calls=%fused_computation.61 | convolution fusion | flops 370968576 | bytes 991232 | tf_op jit(solution)/shard_map/kr,crq->ckq/dot_general | solution.py:61
  352.9 32.3 %fusion.60 = bf16[1,1,1408,88]{2,3,1,0:T(8,128)(2,1)S(1)} fusion(f32[88,1408]{1,0:T(8,128)S(1)} %fusion.17, bf16[1408,88]{0,1:T(8,128)(2,1)S(1)} %reshape.221), kind=kOutput, calls=%fused_computation.60 | convolution fusion | flops 370968576 | bytes 991232 | tf_op jit(solution)/shard_map/kr,crq->ckq/dot_general | solution.py:58
  385.1 32.3 %fusion.19 = f32[88,1408]{1,0:T(8,128)S(1)} fusion(bf16[1408,88]{0,1:T(8,128)(2,1)S(1)} %reshape.217), kind=kOutput, calls=%fused_computation.19 | convolution fusion | flops 370720768 | bytes 743424 | tf_op jit(solution)/shard_map/kr,crq->ckq/dot_general | solution.py:59
  417.4 32.1 %fusion.20 = f32[88,1408]{1,0:T(8,128)S(1)} fusion(bf16[1408,88]{0,1:T(8,128)(2,1)S(1)} %reshape.216), kind=kOutput, calls=%fused_computation.20 | convolution fusion | flops 370720768 | bytes 743424 | tf_op jit(solution)/shard_map/kr,crq->ckq/dot_general | solution.py:56
  449.5 32.3 %fusion.59 = bf16[1,1,1408,88]{2,3,1,0:T(8,128)(2,1)S(1)} fusion(f32[88,1408]{1,0:T(8,128)S(1)} %fusion.19, bf16[1408,88]{0,1:T(8,128)(2,1)S(1)} %reshape.216), kind=kOutput, calls=%fused_computation.59 | convolution fusion | flops 370968576 | bytes 991232 | tf_op jit(solution)/shard_map/kr,crq->ckq/dot_general | solution.py:61
  481.7 32.3 %fusion.58 = bf16[1,1,1408,88]{2,3,1,0:T(8,128)(2,1)S(1)} fusion(f32[88,1408]{1,0:T(8,128)S(1)} %fusion.20, bf16[1408,88]{0,1:T(8,128)(2,1)S(1)} %reshape.217), kind=kOutput, calls=%fused_computation.58 | convolution fusion | flops 370968576 | bytes 991232 | tf_op jit(solution)/shard_map/kr,crq->ckq/dot_general | solution.py:58
  514.0 32.5 %fusion.13 = f32[88,1408]{1,0:T(8,128)S(1)} fusion(bf16[1408,88]{0,1:T(8,128)(2,1)S(1)} %reshape.225), kind=kOutput, calls=%fused_computation.13 | convolution fusion | flops 370720768 | bytes 743424 | tf_op jit(solution)/shard_map/kr,crq->ckq/dot_general | solution.py:59
  546.5 32.1 %fusion.14 = f32[88,1408]{1,0:T(8,128)S(1)} fusion(bf16[1408,88]{0,1:T(8,128)(2,1)S(1)} %reshape.224), kind=kOutput, calls=%fused_computation.14 | convolution fusion | flops 370720768 | bytes 743424 | tf_op jit(solution)/shard_map/kr,crq->ckq/dot_general | solution.py:56
  578.6 32.3 %fusion.63 = bf16[1,1,1408,88]{2,3,1,0:T(8,128)(2,1)S(1)} fusion(f32[88,1408]{1,0:T(8,128)S(1)} %fusion.13, bf16[1408,88]{0,1:T(8,128)(2,1)S(1)} %reshape.224), kind=kOutput, calls=%fused_computation.63 | convolution fusion | flops 370968576 | bytes 991232 | tf_op jit(solution)/shard_map/kr,crq->ckq/dot_general | solution.py:61
  610.8 32.4 %fusion.62 = bf16[1,1,1408,88]{2,3,1,0:T(8,128)(2,1)S(1)} fusion(f32[88,1408]{1,0:T(8,128)S(1)} %fusion.14, bf16[1408,88]{0,1:T(8,128)(2,1)S(1)} %reshape.225), kind=kOutput, calls=%fused_computation.62 | convolution fusion | flops 370968576 | bytes 991232 | tf_op jit(solution)/shard_map/kr,crq->ckq/dot_general | solution.py:58
  646.8 31.0 %collective-permute-done = bf16[2,3,1408,88]{2,3,1,0:T(8,128)(2,1)S(1)} collective-permute-done((bf16[2,3,1408,88]{2,3,1,0:T(8,128)(2,1)S(1)}, bf16[2,3,1408,88]{2,3,1,0:T(8,128)(2,1)S(1)}, u32[]{:S(2)}, u32[]{:S(2)}) %collective-permute-start) | collective-permute-done | bytes 1486880 | tf_op jit(solution)/shard_map/ppermute | solution.py:12
  681.7 32.2 %collective-permute-done.1 = bf16[2,3,1408,88]{2,3,1,0:T(8,128)(2,1)S(1)} collective-permute-done((bf16[2,3,1408,88]{2,3,1,0:T(8,128)(2,1)S(1)}, bf16[2,3,1408,88]{2,3,1,0:T(8,128)(2,1)S(1)}, u32[]{:S(2)}, u32[]{:S(2)}) %collective-permute-start.1) | collective-permute-done | bytes 1486880 | tf_op jit(solution)/shard_map/ppermute | solution.py:12
  717.9 31.4 %collective-permute-done.2 = bf16[2,3,1408,88]{2,3,1,0:T(8,128)(2,1)S(1)} collective-permute-done((bf16[2,3,1408,88]{2,3,1,0:T(8,128)(2,1)S(1)}, bf16[2,3,1408,88]{2,3,1,0:T(8,128)(2,1)S(1)}, u32[]{:S(2)}, u32[]{:S(2)}) %collective-permute-start.2) | collective-permute-done | bytes 1486880 | tf_op jit(solution)/shard_map/ppermute | solution.py:12
  753.5 30.5 %collective-permute-done.3 = bf16[2,3,1408,88]{2,3,1,0:T(8,128)(2,1)S(1)} collective-permute-done((bf16[2,3,1408,88]{2,3,1,0:T(8,128)(2,1)S(1)}, bf16[2,3,1408,88]{2,3,1,0:T(8,128)(2,1)S(1)}, u32[]{:S(2)}, u32[]{:S(2)}) %collective-permute-start.3) | collective-permute-done | bytes 1486880 | tf_op jit(solution)/shard_map/ppermute | solution.py:12
  788.2 29.6 %collective-permute-done.4 = bf16[2,3,1408,88]{2,3,1,0:T(8,128)(2,1)S(1)} collective-permute-done((bf16[2,3,1408,88]{2,3,1,0:T(8,128)(2,1)S(1)}, bf16[2,3,1408,88]{2,3,1,0:T(8,128)(2,1)S(1)}, u32[]{:S(2)}, u32[]{:S(2)}) %collective-permute-start.4) | collective-permute-done | bytes 1486880 | tf_op jit(solution)/shard_map/ppermute | solution.py:12
  822.9 28.7 %collective-permute-done.5 = bf16[2,3,1408,88]{2,3,1,0:T(8,128)(2,1)S(1)} collective-permute-done((bf16[2,3,1408,88]{2,3,1,0:T(8,128)(2,1)S(1)}, bf16[2,3,1408,88]{2,3,1,0:T(8,128)(2,1)S(1)}, u32[]{:S(2)}, u32[]{:S(2)}) %collective-permute-start.5) | collective-permute-done | bytes 1486880 | tf_op jit(solution)/shard_map/ppermute | solution.py:12
  857.9 27.7 %collective-permute-done.6 = bf16[2,3,1408,88]{2,3,1,0:T(8,128)(2,1)S(1)} collective-permute-done((bf16[2,3,1408,88]{2,3,1,0:T(8,128)(2,1)S(1)}, bf16[2,3,1408,88]{2,3,1,0:T(8,128)(2,1)S(1)}, u32[]{:S(2)}, u32[]{:S(2)}) %collective-permute-start.6) | collective-permute-done | bytes 1486880 | tf_op jit(solution)/shard_map/ppermute | solution.py:12
  891.9 26.8 %collective-permute-done.7 = bf16[2,3,1408,88]{2,3,1,0:T(8,128)(2,1)S(1)} collective-permute-done((bf16[2,3,1408,88]{2,3,1,0:T(8,128)(2,1)S(1)}, bf16[2,3,1408,88]{2,3,1,0:T(8,128)(2,1)S(1)}, u32[]{:S(2)}, u32[]{:S(2)}) %collective-permute-start.7) | collective-permute-done | bytes 1486880 | tf_op jit(solution)/shard_map/ppermute | solution.py:12
  925.1 25.9 %collective-permute-done.8 = bf16[2,3,1408,88]{2,3,1,0:T(8,128)(2,1)S(1)} collective-permute-done((bf16[2,3,1408,88]{2,3,1,0:T(8,128)(2,1)S(1)}, bf16[2,3,1408,88]{2,3,1,0:T(8,128)(2,1)S(1)}, u32[]{:S(2)}, u32[]{:S(2)}) %collective-permute-start.8) | collective-permute-done | bytes 1486880 | tf_op jit(solution)/shard_map/ppermute | solution.py:12
  958.3 23.9 %collective-permute-done.9 = bf16[2,3,1408,88]{2,3,1,0:T(8,128)(2,1)} collective-permute-done((bf16[2,3,1408,88]{2,3,1,0:T(8,128)(2,1)S(1)}, bf16[2,3,1408,88]{2,3,1,0:T(8,128)(2,1)}, u32[]{:S(2)}, u32[]{:S(2)}) %collective-permute-start.9) | collective-permute-done | bytes 1486880 | tf_op jit(solution)/shard_map/ppermute | solution.py:12
  988.5 24.8 %collective-permute-done.10 = bf16[2,3,1408,88]{2,3,1,0:T(8,128)(2,1)S(1)} collective-permute-done((bf16[2,3,1408,88]{2,3,1,0:T(8,128)(2,1)}, bf16[2,3,1408,88]{2,3,1,0:T(8,128)(2,1)S(1)}, u32[]{:S(2)}, u32[]{:S(2)}) %collective-permute-start.10) | collective-permute-done | bytes 1486880 | tf_op jit(solution)/shard_map/ppermute | solution.py:12
  1019.7 24.7 %collective-permute-done.11 = bf16[2,3,1408,88]{2,3,1,0:T(8,128)(2,1)S(1)} collective-permute-done((bf16[2,3,1408,88]{2,3,1,0:T(8,128)(2,1)S(1)}, bf16[2,3,1408,88]{2,3,1,0:T(8,128)(2,1)S(1)}, u32[]{:S(2)}, u32[]{:S(2)}) %collective-permute-start.11) | collective-permute-done | bytes 1486880 | tf_op jit(solution)/shard_map/ppermute | solution.py:12
  1053.0 22.2 %collective-permute-done.12 = bf16[2,3,1408,88]{2,3,1,0:T(8,128)(2,1)S(1)} collective-permute-done((bf16[2,3,1408,88]{2,3,1,0:T(8,128)(2,1)S(1)}, bf16[2,3,1408,88]{2,3,1,0:T(8,128)(2,1)S(1)}, u32[]{:S(2)}, u32[]{:S(2)}) %collective-permute-start.12) | collective-permute-done | bytes 1486880 | tf_op jit(solution)/shard_map/ppermute | solution.py:12
  1177.4 145.4 %all-reduce.3.cloned.1.call-done = bf16[2,4,3,1408,88]{3,1,4,2,0:T(4,128)(2,1)} async-done(((bf16[2,4,3,1408,88]{3,1,4,2,0:T(4,128)(2,1)}), bf16[2,4,3,1408,88]{3,1,4,2,0:T(4,128)(2,1)}) %all-reduce.3.cloned.1.call-update) | async-done | bytes 5947408
  (116 shorter events, 232.6 us)
Async XLA Ops:
  74.9 77.0 %all-to-all-start.2 = ((bf16[2,1,88,1408]{2,0,1,3:T(2,128)(2,1)}), bf16[2,1,88,1408]{2,0,1,3:T(2,128)(2,1)S(1)}, u32[]{:S(2)}, u32[]{:S(2)}) async-start(bf16[2,1,88,1408]{2,0,1,3:T(2,128)(2,1)} %copy.23), calls=%async_computation.2 | async-start | bytes 1441792 | tf_op jit(solution)/shard_map/all_to_all | solution.py:53
  151.9 74.5 %all-to-all-start.1 = ((bf16[2,1,88,1408]{2,0,1,3:T(2,128)(2,1)}), bf16[2,1,88,1408]{2,0,1,3:T(2,128)(2,1)S(1)}, u32[]{:S(2)}, u32[]{:S(2)}) async-start(bf16[2,1,88,1408]{2,0,1,3:T(2,128)(2,1)} %copy.21), calls=%async_computation.1 | async-start | bytes 1441792 | tf_op jit(solution)/shard_map/all_to_all | solution.py:53
  226.4 28.6 %all-to-all-start = ((bf16[2,1,88,1408]{2,0,1,3:T(2,128)(2,1)}), bf16[2,1,88,1408]{2,0,1,3:T(2,128)(2,1)S(1)}, u32[]{:S(2)}, u32[]{:S(2)}) async-start(bf16[2,1,88,1408]{2,0,1,3:T(2,128)(2,1)} %copy.19), calls=%async_computation | async-start | bytes 1441792 | tf_op jit(solution)/shard_map/all_to_all | solution.py:53
  233.6 1089.2 %all-reduce.3.cloned.1.call-start = ((), (), s32[]{:S(2)}) async-start(), calls=%async_computation.3 | async-start | bytes 11894784
  643.6 34.2 %collective-permute-start = (bf16[2,3,1408,88]{2,3,1,0:T(8,128)(2,1)S(1)}, bf16[2,3,1408,88]{2,3,1,0:T(8,128)(2,1)S(1)}, u32[]{:S(2)}, u32[]{:S(2)}) collective-permute-start(bf16[2,3,1408,88]{2,3,1,0:T(8,128)(2,1)S(1)} %get-tuple-element.51), channel_id=1, source_target_pairs={{0,16},{16,32},{32,48},{48,64},{64,80},{80,96},{96,112},{112,128},... | collective-permute-start | bytes 4460552 | tf_op jit(solution)/shard_map/ppermute | solution.py:12
  677.8 36.1 %collective-permute-start.1 = (bf16[2,3,1408,88]{2,3,1,0:T(8,128)(2,1)S(1)}, bf16[2,3,1408,88]{2,3,1,0:T(8,128)(2,1)S(1)}, u32[]{:S(2)}, u32[]{:S(2)}) collective-permute-start(bf16[2,3,1408,88]{2,3,1,0:T(8,128)(2,1)S(1)} %collective-permute-done), channel_id=1, source_target_pairs={{0,16},{16,32},{32,48},{48,64},{64,80},{80,96},{96,112},{112,128},... | collective-permute-start | bytes 4460552 | tf_op jit(solution)/shard_map/ppermute | solution.py:12
  713.9 35.4 %collective-permute-start.2 = (bf16[2,3,1408,88]{2,3,1,0:T(8,128)(2,1)S(1)}, bf16[2,3,1408,88]{2,3,1,0:T(8,128)(2,1)S(1)}, u32[]{:S(2)}, u32[]{:S(2)}) collective-permute-start(bf16[2,3,1408,88]{2,3,1,0:T(8,128)(2,1)S(1)} %collective-permute-done.1), channel_id=1, source_target_pairs={{0,16},{16,32},{32,48},{48,64},{64,80},{80,96},{96,112},{112,128},... | collective-permute-start | bytes 4460552 | tf_op jit(solution)/shard_map/ppermute | solution.py:12
  749.3 34.7 %collective-permute-start.3 = (bf16[2,3,1408,88]{2,3,1,0:T(8,128)(2,1)S(1)}, bf16[2,3,1408,88]{2,3,1,0:T(8,128)(2,1)S(1)}, u32[]{:S(2)}, u32[]{:S(2)}) collective-permute-start(bf16[2,3,1408,88]{2,3,1,0:T(8,128)(2,1)S(1)} %collective-permute-done.2), channel_id=1, source_target_pairs={{0,16},{16,32},{32,48},{48,64},{64,80},{80,96},{96,112},{112,128},... | collective-permute-start | bytes 4460552 | tf_op jit(solution)/shard_map/ppermute | solution.py:12
  784.0 33.8 %collective-permute-start.4 = (bf16[2,3,1408,88]{2,3,1,0:T(8,128)(2,1)S(1)}, bf16[2,3,1408,88]{2,3,1,0:T(8,128)(2,1)S(1)}, u32[]{:S(2)}, u32[]{:S(2)}) collective-permute-start(bf16[2,3,1408,88]{2,3,1,0:T(8,128)(2,1)S(1)} %collective-permute-done.3), channel_id=1, source_target_pairs={{0,16},{16,32},{32,48},{48,64},{64,80},{80,96},{96,112},{112,128},... | collective-permute-start | bytes 4460552 | tf_op jit(solution)/shard_map/ppermute | solution.py:12
  817.8 33.8 %collective-permute-start.5 = (bf16[2,3,1408,88]{2,3,1,0:T(8,128)(2,1)S(1)}, bf16[2,3,1408,88]{2,3,1,0:T(8,128)(2,1)S(1)}, u32[]{:S(2)}, u32[]{:S(2)}) collective-permute-start(bf16[2,3,1408,88]{2,3,1,0:T(8,128)(2,1)S(1)} %collective-permute-done.4), channel_id=1, source_target_pairs={{0,16},{16,32},{32,48},{48,64},{64,80},{80,96},{96,112},{112,128},... | collective-permute-start | bytes 4460552 | tf_op jit(solution)/shard_map/ppermute | solution.py:12
  851.6 34.0 %collective-permute-start.6 = (bf16[2,3,1408,88]{2,3,1,0:T(8,128)(2,1)S(1)}, bf16[2,3,1408,88]{2,3,1,0:T(8,128)(2,1)S(1)}, u32[]{:S(2)}, u32[]{:S(2)}) collective-permute-start(bf16[2,3,1408,88]{2,3,1,0:T(8,128)(2,1)S(1)} %collective-permute-done.5), channel_id=1, source_target_pairs={{0,16},{16,32},{32,48},{48,64},{64,80},{80,96},{96,112},{112,128},... | collective-permute-start | bytes 4460552 | tf_op jit(solution)/shard_map/ppermute | solution.py:12
  885.6 33.1 %collective-permute-start.7 = (bf16[2,3,1408,88]{2,3,1,0:T(8,128)(2,1)S(1)}, bf16[2,3,1408,88]{2,3,1,0:T(8,128)(2,1)S(1)}, u32[]{:S(2)}, u32[]{:S(2)}) collective-permute-start(bf16[2,3,1408,88]{2,3,1,0:T(8,128)(2,1)S(1)} %collective-permute-done.6), channel_id=1, source_target_pairs={{0,16},{16,32},{32,48},{48,64},{64,80},{80,96},{96,112},{112,128},... | collective-permute-start | bytes 4460552 | tf_op jit(solution)/shard_map/ppermute | solution.py:12
  918.8 32.2 %collective-permute-start.8 = (bf16[2,3,1408,88]{2,3,1,0:T(8,128)(2,1)S(1)}, bf16[2,3,1408,88]{2,3,1,0:T(8,128)(2,1)S(1)}, u32[]{:S(2)}, u32[]{:S(2)}) collective-permute-start(bf16[2,3,1408,88]{2,3,1,0:T(8,128)(2,1)S(1)} %collective-permute-done.7), channel_id=1, source_target_pairs={{0,16},{16,32},{32,48},{48,64},{64,80},{80,96},{96,112},{112,128},... | collective-permute-start | bytes 4460552 | tf_op jit(solution)/shard_map/ppermute | solution.py:12
  951.0 31.3 %collective-permute-start.9 = (bf16[2,3,1408,88]{2,3,1,0:T(8,128)(2,1)S(1)}, bf16[2,3,1408,88]{2,3,1,0:T(8,128)(2,1)}, u32[]{:S(2)}, u32[]{:S(2)}) collective-permute-start(bf16[2,3,1408,88]{2,3,1,0:T(8,128)(2,1)S(1)} %collective-permute-done.8), channel_id=1, source_target_pairs={{0,16},{16,32},{32,48},{48,64},{64,80},{80,96},{96,112},{112,128},... | collective-permute-start | bytes 4460552 | tf_op jit(solution)/shard_map/ppermute | solution.py:12
  982.2 31.1 %collective-permute-start.10 = (bf16[2,3,1408,88]{2,3,1,0:T(8,128)(2,1)}, bf16[2,3,1408,88]{2,3,1,0:T(8,128)(2,1)S(1)}, u32[]{:S(2)}, u32[]{:S(2)}) collective-permute-start(bf16[2,3,1408,88]{2,3,1,0:T(8,128)(2,1)} %collective-permute-done.9), channel_id=1, source_target_pairs={{0,16},{16,32},{32,48},{48,64},{64,80},{80,96},{96,112},{112,128},... | collective-permute-start | bytes 4460552 | tf_op jit(solution)/shard_map/ppermute | solution.py:12
  1013.4 38.1 %copy-start.10 = (bf16[2,3,1408,88]{2,3,1,0:T(8,128)(2,1)}, bf16[2,3,1408,88]{2,3,1,0:T(8,128)(2,1)S(1)}, u32[]{:S(2)}) copy-start(bf16[2,3,1408,88]{2,3,1,0:T(8,128)(2,1)S(1)} %collective-permute-done.10) | copy-start | bytes 4460548
  1013.4 31.0 %collective-permute-start.11 = (bf16[2,3,1408,88]{2,3,1,0:T(8,128)(2,1)S(1)}, bf16[2,3,1408,88]{2,3,1,0:T(8,128)(2,1)S(1)}, u32[]{:S(2)}, u32[]{:S(2)}) collective-permute-start(bf16[2,3,1408,88]{2,3,1,0:T(8,128)(2,1)S(1)} %collective-permute-done.10), channel_id=1, source_target_pairs={{0,16},{16,32},{32,48},{48,64},{64,80},{80,96},{96,112},{112,128},... | collective-permute-start | bytes 4460552 | tf_op jit(solution)/shard_map/ppermute | solution.py:12
  1044.4 7.1 copy-start.9
  1044.4 30.8 %collective-permute-start.12 = (bf16[2,3,1408,88]{2,3,1,0:T(8,128)(2,1)S(1)}, bf16[2,3,1408,88]{2,3,1,0:T(8,128)(2,1)S(1)}, u32[]{:S(2)}, u32[]{:S(2)}) collective-permute-start(bf16[2,3,1408,88]{2,3,1,0:T(8,128)(2,1)S(1)} %collective-permute-done.11), channel_id=1, source_target_pairs={{0,16},{16,32},{32,48},{48,64},{64,80},{80,96},{96,112},{112,128},... | collective-permute-start | bytes 4460552 | tf_op jit(solution)/shard_map/ppermute | solution.py:12
  1075.2 31.1 %collective-permute-start.13 = (bf16[2,3,1408,88]{2,3,1,0:T(8,128)(2,1)S(1)}, bf16[2,3,1408,88]{2,3,1,0:T(8,128)(2,1)}, u32[]{:S(2)}, u32[]{:S(2)}) collective-permute-start(bf16[2,3,1408,88]{2,3,1,0:T(8,128)(2,1)S(1)} %collective-permute-done.12), channel_id=1, source_target_pairs={{0,16},{16,32},{32,48},{48,64},{64,80},{80,96},{96,112},{112,128},... | collective-permute-start | bytes 4460552 | tf_op jit(solution)/shard_map/ppermute | solution.py:12
  1106.3 31.1 %collective-permute-start.14 = (bf16[2,3,1408,88]{2,3,1,0:T(8,128)(2,1)}, bf16[2,3,1408,88]{2,3,1,0:T(8,128)(2,1)}, u32[]{:S(2)}, u32[]{:S(2)}) collective-permute-start(bf16[2,3,1408,88]{2,3,1,0:T(8,128)(2,1)} %collective-permute-done.13), channel_id=1, source_target_pairs={{0,16},{16,32},{32,48},{48,64},{64,80},{80,96},{96,112},{112,128},... | collective-permute-start | bytes 4460552 | tf_op jit(solution)/shard_map/ppermute | solution.py:12
  1139.0 2.6 copy-start.6
  1141.5 2.5 copy-start.7
  1141.5 2.5 copy-start.8
  1145.3 2.5 copy-start.5
  1146.5 2.5 copy-start.3
  1146.5 2.5 copy-start.4
  1147.8 2.6 copy-start.1
  1147.8 2.6 copy-start.2
  1149.0 2.6 copy-start
  1160.3 2.5 copy-start.11
  1175.5 0.7 copy-start.12
Sparse Core Ops, SparseCore 0:
  1175.7 147.1 all-reduce.2
where the time goes:
time: 1340 us; the launch traced here: 1330 us
  matrix products  594 us (44%)
  waiting for transfers between devices  554 us (41%)
  starting transfers between devices  110 us (8%)
  other arithmetic  48.2 us (4%)
  between operations  14.8 us (1%)
    ppermute x15, waiting for transfers between devices, from_behind(): lax.ppermute(value, axis, [(source, source + steps) for source in range(f...  389 us
    unnamed x2, waiting for transfers between devices  145 us
    dot_general x3, matrix products, on_device(): jnp.dot(flattened, sine_cols, preferred_element_type=jnp.float32)  97.4 us
    dot_general x3, matrix products, on_device(): jnp.einsum('kr,crq->ckq', cosine_rows, imag_part, preferred_element_type=...  97 us
    dot_general x3, matrix products, on_device(): jnp.einsum('kr,crq->ckq', sine_rows, imag_part, preferred_element_type=jn...  96.9 us
    dot_general x3, matrix products, on_device(): jnp.einsum('kr,crq->ckq', sine_rows, real_part, preferred_element_type=jn...  96.8 us
    dot_general x3, matrix products, on_device(): jnp.dot(flattened, cosine_cols, preferred_element_type=jnp.float32)  96.7 us
    dot_general x3, matrix products, on_device(): jnp.einsum('kr,crq->ckq', cosine_rows, real_part, preferred_element_type=...  96.2 us
  transfers between devices with their start and end apart: 19, of which 17 were waited for; matrix products, arithmetic and copies ran while one was open for 12% of the time, Pallas kernels for 0%

commit v1 on v0

v1 whole, which is shorter than its diff:
```python
import functools
import math

import jax
import jax.numpy as jnp
import ml_dtypes
import numpy as np
from jax import lax
from jax.experimental import pallas as pl
from jax.experimental.pallas import tpu as pltpu
from jax.sharding import PartitionSpec as P

F32 = jnp.float32
BF16 = jnp.bfloat16
LANES = 128
GROUP = 16


def phase(numbers, length):
    return (numbers % length) * (2.0 * math.pi / length)


def column_table(length, parts, half, width):
    block = length // parts
    kx = (np.arange(parts)[:, None] * block + np.arange(half)[None, :]) % length
    angles = phase(np.arange(length)[:, None, None] * kx[None], length)
    table = np.zeros((length, parts, LANES))
    table[:, :, :half] = np.cos(angles)
    table[:, :, half:width] = -np.sin(angles)
    return (table / math.sqrt(length)).reshape(length, parts * LANES).astype(ml_dtypes.bfloat16)


def row_table(length, parts, rows_up, row_order):
    block = length // parts
    ky = np.arange(parts // 2)[:, None] * block + np.arange(block + 1)[None, :]
    angles = phase(ky[:, :, None] * row_order[None, None, :], length)
    table = np.zeros((parts // 2, 2, rows_up, row_order.size))
    table[:, 0, : block + 1] = np.cos(angles)
    table[:, 1, : block + 1] = np.sin(angles)
    return (table / math.sqrt(length)).reshape(-1, row_order.size).astype(ml_dtypes.bfloat16)


def lane_index(shape):
    return lax.broadcasted_iota(jnp.int32, shape, len(shape) - 1)


def pack(groups, width, tiles):
    lane = lane_index((GROUP, LANES))
    out = [None] * tiles

    def put(tile, value):
        out[tile] = value if out[tile] is None else out[tile] + value

    for number, value in enumerate(groups):
        tile, shift = divmod(number * width, LANES)
        if shift:
            value = pltpu.roll(value, shift, 1)
        if shift + width <= LANES:
            put(tile, value)
        else:
            put(tile, jnp.where(lane >= shift, value, 0.0))
            put(tile + 1, jnp.where(lane < shift, value, 0.0))
    return jnp.concatenate(out, axis=1)


def unpack(load, number, width, rows):
    lane = lane_index((rows, LANES))
    tile, shift = divmod(number * width, LANES)
    value = load(tile)
    if shift + width > LANES:
        value = jnp.where(lane >= shift, value, load(tile + 1))
    if shift:
        value = pltpu.roll(value, LANES - shift, 1)
    return jnp.where(lane < width, value, 0.0)


def column_kernel(width, x_ref, mask_ref, table_ref, out_ref, left):
    channels, rows = x_ref.shape[1], x_ref.shape[2]
    whole = rows // GROUP * GROUP

    @pl.when(pl.program_id(0) == 0)
    def _():
        masked = [x_ref[0, c].astype(F32) * mask_ref[0, c].astype(F32) for c in range(channels)]
        pieces = [value[:whole] for value in masked] + [value[whole:] for value in masked]
        used = channels * rows
        if left.shape[0] > used:
            pieces.append(jnp.zeros((left.shape[0] - used, left.shape[1]), F32))
        left[...] = jnp.concatenate(pieces, axis=0).astype(BF16)

    result = jnp.dot(left[...], table_ref[...], preferred_element_type=F32)
    for part in range(out_ref.shape[0]):
        lanes = slice(part * LANES, (part + 1) * LANES)
        groups = [result[g * GROUP : (g + 1) * GROUP, lanes] for g in range(left.shape[0] // GROUP)]
        out_ref[part] = pack(groups, width, out_ref.shape[2] // LANES).astype(BF16)


def row_kernel(width, channels, rows_up, x_ref, table_ref, out_ref, right):
    half = width // 2
    parts = x_ref.shape[0]
    depth = parts * GROUP
    steps = right.shape[0] // depth
    step = pl.program_id(0)

    @pl.when(step == 0)
    def _():
        def load(tile):
            return x_ref[:, :, tile * LANES : (tile + 1) * LANES].reshape(depth, LANES).astype(F32)

        row_in_group = lax.broadcasted_iota(jnp.int32, (depth, LANES), 0) % GROUP
        for c in range(channels):
            lanes = slice(c * LANES, (c + 1) * LANES)
            for a in range(steps - 1):
                value = unpack(load, c * (steps - 1) + a, width, depth)
                right[a * depth : (a + 1) * depth, lanes] = value.astype(BF16)
            value = unpack(load, channels * (steps - 1) + c // 2, width, depth)
            value = jnp.where((row_in_group >= GROUP // 2) == (c % 2 == 1), value, 0.0)
            right[(steps - 1) * depth :, lanes] = value.astype(BF16)

    result = jnp.dot(table_ref[...], right[...], preferred_element_type=F32)
    lane = lane_index((rows_up, LANES))
    blocks = table_ref.shape[0] // (2 * rows_up)
    for b in range(blocks):
        plus, minus = [], []
        for c in range(channels):
            lanes = slice(c * LANES, (c + 1) * LANES)
            top = 2 * b * rows_up
            even = result[top : top + rows_up, lanes]
            odd = result[top + rows_up : top + 2 * rows_up, lanes]
            turned = jnp.where(
                lane < half,
                pltpu.roll(odd, LANES - half, 1),
                jnp.where(lane < width, -pltpu.roll(odd, half, 1), 0.0),
            )
            plus.append(even + turned)
            minus.append(even - turned)
        for value, place in ((plus, step * blocks + b), (minus, parts - 1 - step * blocks - b)):
            groups = [v[a : a + GROUP] for v in value for a in range(0, rows_up, GROUP)]
            out_ref[place] = pack(groups, width, out_ref.shape[2] // LANES).astype(BF16)


def lag_kernel(half, lag_ref, z_ref, first_ref, out_ref, wide, swapped):
    slots, rows, lanes = z_ref.shape
    first = first_ref[...] > 0.0

    def swap(value):
        return jnp.where(first, pltpu.roll(value, lanes - half, 1), pltpu.roll(value, half, 1))

    for t in range(slots):
        value = z_ref[t].astype(F32)
        wide[t] = value
        swapped[t] = swap(value)
    for entry in range(out_ref.shape[0]):
        lag = lag_ref[entry]

        def add(t, sums):
            later = wide[t + lag]
            return sums[0] + wide[t] * later, sums[1] + swapped[t] * later

        zero = jnp.zeros((rows, lanes), F32)
        real, imag = lax.fori_loop(0, slots - lag, add, (zero, zero))
        value = jnp.where(first, real + swap(real), swap(imag) - imag)
        out_ref[entry] = (value / (slots - lag).astype(F32)).astype(BF16)


def place_kernel(width, channels, rows_up, own_ref, other_ref, spread_ref, out_ref):
    block = out_ref.shape[3]
    per = rows_up // GROUP
    at_row = lax.broadcasted_iota(jnp.int32, (rows_up, rows_up), 0)
    at_col = lax.broadcasted_iota(jnp.int32, (rows_up, rows_up), 1)
    back = lax.axis_index("slot") * 2 >= lax.axis_size("slot")
    source = jnp.where(back, block - at_row, at_row)
    order = (source == at_col).astype(F32).astype(BF16)
    for entry in range(out_ref.shape[1]):
        for c in range(channels):
            sides = []
            for ref in (own_ref, other_ref):
                def load(tile):
                    return ref[entry, :, tile * LANES : (tile + 1) * LANES].astype(F32)

                sides.append(
                    jnp.concatenate([unpack(load, c * per + a, width, GROUP) for a in range(per)], axis=0)
                )
            both = jnp.concatenate(sides, axis=1).astype(BF16)
            spread = jnp.dot(both, spread_ref[...], preferred_element_type=F32).astype(BF16)
            placed = jnp.dot(order, spread, preferred_element_type=F32)
            out_ref[0, entry, c] = placed[:block, :block]
            out_ref[1, entry, c] = placed[:block, LANES : LANES + block]


def spread_table(block, half):
    table = np.zeros((2 * LANES, 2 * LANES))
    for j in range(block):
        if j < half:
            table[j, j] = 1.0
            table[half + j, LANES + j] = 1.0
        else:
            table[LANES + block - j, j] = 1.0
            table[LANES + half + block - j, LANES + j] = -1.0
    return table.astype(ml_dtypes.bfloat16)


def up(value, unit):
    return -(-value // unit) * unit


def on_device(slots, parts, innovation, clear_mask, lag_list):
    _, channels, rows, cols = innovation.shape
    length = rows * parts
    block = cols // parts
    half = block // 2 + 1
    width = 2 * half
    entries = lag_list.shape[0]
    limit = pltpu.CompilerParams(vmem_limit_bytes=40 * 2**20)

    left_rows = up(channels * rows, GROUP)
    packed = up(left_rows // GROUP * width, LANES)
    per_step = 4
    g = pl.pallas_call(
        functools.partial(column_kernel, width),
        grid=(parts // per_step,),
        in_specs=[
            pl.BlockSpec(innovation.shape, lambda i: (0, 0, 0, 0)),
            pl.BlockSpec(clear_mask.shape, lambda i: (0, 0, 0, 0)),
            pl.BlockSpec((cols, per_step * LANES), lambda i: (0, i)),
        ],
        out_specs=pl.BlockSpec((per_step, GROUP, packed), lambda i: (i, 0, 0)),
        out_shape=jax.ShapeDtypeStruct((parts, GROUP, packed), BF16),
        scratch_shapes=[pltpu.VMEM((left_rows, cols), BF16)],
        compiler_params=limit,
        name="columns",
    )(innovation, clear_mask, jnp.asarray(column_table(cols, parts, half, width)))
    g = lax.all_to_all(g, "row", 0, 0, tiled=True)

    whole = rows // GROUP
    order = [
        p * rows + (a * GROUP + b if a < whole else whole * GROUP + b % (GROUP // 2))
        for a in range(whole + 1)
        for p in range(parts)
        for b in range(GROUP)
    ]
    ky_block = length // slots
    rows_up = up(ky_block + 1, GROUP)
    table = row_table(length, slots, rows_up, np.array(order))
    packed = up(rows_up // GROUP * channels * width, LANES)
    row_steps = 2
    f = pl.pallas_call(
        functools.partial(row_kernel, width, channels, rows_up),
        grid=(row_steps,),
        in_specs=[
            pl.BlockSpec(g.shape, lambda i: (0, 0, 0)),
            pl.BlockSpec((table.shape[0] // row_steps, table.shape[1]), lambda i: (i, 0)),
        ],
        out_specs=pl.BlockSpec((slots, GROUP, packed), lambda i: (0, 0, 0)),
        out_shape=jax.ShapeDtypeStruct((slots, GROUP, packed), BF16),
        scratch_shapes=[pltpu.VMEM((table.shape[1], channels * LANES), BF16)],
        compiler_params=limit,
        name="rows",
    )(g, jnp.asarray(table))
    f = lax.all_to_all(f, "slot", 0, 0, tiled=True)

    first = np.broadcast_to((np.arange(packed) % width < half).astype(np.float32), (GROUP, packed))
    own = pl.pallas_call(
        functools.partial(lag_kernel, half),
        in_specs=[
            pl.BlockSpec(memory_space=pltpu.SMEM),
            pl.BlockSpec(memory_space=pltpu.VMEM),
            pl.BlockSpec(memory_space=pltpu.VMEM),
        ],
        out_specs=pl.BlockSpec(memory_space=pltpu.VMEM),
        out_shape=jax.ShapeDtypeStruct((entries, GROUP, packed), BF16),
        scratch_shapes=[pltpu.VMEM((slots, GROUP, packed), F32)] * 2,
        compiler_params=limit,
        name="lags",
    )(lag_list, f, jnp.asarray(first))

    mirror = [
        (s * parts + p, (slots - 1 - s) * parts + parts - 1 - p) for s in range(slots) for p in range(parts)
    ]
    other = lax.ppermute(own, ("slot", "row"), mirror)

    return pl.pallas_call(
        functools.partial(place_kernel, width, channels, rows_up),
        in_specs=[pl.BlockSpec(memory_space=pltpu.VMEM)] * 3,
        out_specs=pl.BlockSpec(memory_space=pltpu.VMEM),
        out_shape=jax.ShapeDtypeStruct((2, entries, channels, ky_block, block), F32),
        compiler_params=limit,
        name="place",
    )(own, other, jnp.asarray(spread_table(block, half)))


def solution(mesh):
    placed = (P("slot", None, "row", None), P("slot", None, "row", None), P())
    return jax.shard_map(
        functools.partial(on_device, mesh.shape["slot"], mesh.shape["row"]),
        mesh=mesh,
        in_specs=placed,
        out_specs=P(None, None, None, "slot", "row"),
        check_vma=False,
    )
```

time: 1340 us -> 91.8 us (0.07)
  matrix products: 594 us -> 0 us
  waiting for transfers between devices: 554 us -> 16.4 us
  starting transfers between devices: 110 us -> 1.35 us
  blocking collectives: 0 us -> 54.3 us
  other arithmetic: 48.2 us -> 0 us
  between operations: 14.8 us -> 0.06 us
  Pallas kernels: 0 us -> 14.5 us
    dot_general x19 -> x0, matrix products: 594 us -> none  [the longest x3 97.4 us: on_device(): jnp.dot(flattened, sine_cols, preferred_element_type=jnp.float32)]
    ppermute x15 -> x1, waiting for transfers between devices: 389 us -> 16.4 us  [on_device(): other = lax.ppermute(own, ('slot', 'row'), mirror)]
    unnamed x2 -> x0, waiting for transfers between devices: 145 us -> none
    ppermute x15 -> x1, starting transfers between devices: 84.7 us -> 1.35 us  [on_device(): other = lax.ppermute(own, ('slot', 'row'), mirror)]
    all_to_all x0 -> x2, blocking collectives: none -> 54.3 us  [the longest x1 32.7 us: on_device(): g = lax.all_to_all(g, 'row', 0, 0, tiled=True)]
    all_to_all x3 -> x0, starting transfers between devices: 25.4 us -> none  [on_device(): lax.all_to_all(channel_block, 'row', split_axis=3, concat_axis=2, tiled=T...]
    convert_element_type x24 -> x0, other arithmetic: 23.7 us -> none  [the longest x8 13.7 us: cross_term(): (early_wide[0] * late_wide[0] + early_wide[1] * late_wide[1]).astype(jnp....]
    unnamed x15 -> x0, other arithmetic: 20 us -> none
  transfers between devices with their start and end apart: 19 -> 1, of which waited for: 17 -> 1; matrix products, arithmetic and copies ran while one was open for 12% -> 0% of each run, Pallas kernels for 0% -> 0%
where the time goes in v1:
time: 91.8 us
  blocking collectives  54.3 us (59%)
  waiting for transfers between devices  16.4 us (18%)
  Pallas kernels  14.5 us (16%)
  local copies, waits for them, and re-layouts  5.16 us (6%)
  starting transfers between devices  1.35 us (1%)
    all_to_all x1, blocking collectives, on_device(): g = lax.all_to_all(g, 'row', 0, 0, tiled=True)  32.7 us
    all_to_all x1, blocking collectives, on_device(): f = lax.all_to_all(f, 'slot', 0, 0, tiled=True)  21.6 us
    ppermute x1, waiting for transfers between devices, on_device(): other = lax.ppermute(own, ('slot', 'row'), mirror)  16.4 us
    unnamed x14, local copies, waits for them, and re-layouts  5.15 us
    pallas_call x1, Pallas kernels, on_device(): pl.pallas_call(functools.partial(row_kernel, width, channels, rows_up), g...  4.18 us
    pallas_call x1, Pallas kernels, on_device(): pl.pallas_call(functools.partial(lag_kernel, half), in_specs=[pl.BlockSpe...  3.71 us
    pallas_call x1, Pallas kernels, on_device(): pl.pallas_call(functools.partial(column_kernel, width), grid=(parts // pe...  3.66 us
    pallas_call x1, Pallas kernels, on_device(): pl.pallas_call(functools.partial(place_kernel, width, channels, rows_up),...  2.99 us
  transfers between devices with their start and end apart: 1, of which 1 were waited for; matrix products, arithmetic and copies ran while one was open for 0% of the time, Pallas kernels for 0%

profile of v1, /device:TPU:1, one launch (start us, length us, event | category | flops | bytes accessed | tf_op | source)
XLA Modules:
  0.0 91.8 jit_solution(3615314057482651967)
XLA Ops:
  0.0 0.0 copy-start
  0.0 2.6 %copy-done = bf16[1408,2048]{1,0:T(8,128)(2,1)S(1)} copy-done((bf16[1408,2048]{1,0:T(8,128)(2,1)S(1)}, bf16[1408,2048]{1,0:T(8,128)(2,1)}, u32[]{:S(2)}) %copy-start) | copy-done | bytes 5767192
  2.6 0.0 copy-start.2
  2.6 1.4 %copy-done.2 = s32[1,3,88,1408]{3,2,1,0:T(8,128)S(1)} copy-done((s32[1,3,88,1408]{3,2,1,0:T(8,128)S(1)}, s32[1,3,88,1408]{3,2,1,0:T(8,128)}, u32[]{:S(2)}) %copy-start.2) | copy-done | bytes 1486872
  4.0 0.0 copy-start.3
  4.0 1.1 %copy-done.3 = bf16[1,3,88,1408]{3,2,1,0:T(8,128)(2,1)S(1)} copy-done((bf16[1,3,88,1408]{3,2,1,0:T(8,128)(2,1)S(1)}, bf16[1,3,88,1408]{3,2,1,0:T(8,128)(2,1)}, u32[]{:S(2)}) %copy-start.3) | copy-done | bytes 743448
  5.1 0.0 copy-start.1
  5.1 3.7 %columns.1 = bf16[16,16,1536]{2,1,0:T(8,128)(2,1)S(1)} custom-call(bf16[1,3,88,1408]{3,2,1,0:T(8,128)(2,1)S(1)} %copy-done.3, s32[1,3,88,1408]{3,2,1,0:T(8,128)S(1)} %copy-done.2, bf16[1408,2048]{1,0:T(8,128)(2,1)S(1)} %copy-done), custom_call_target="tpu_custom_call" | custom-call | tf_op jit(solution)/shard_map/columns/pallas_call | solution.py:218
  8.8 0.0 copy-start.6
  8.8 0.0 copy-start.5
  8.8 32.7 %all_to_all.10.x_ref = bf16[16,16,1536]{2,1,0:T(8,128)(2,1)S(1)} all-to-all(bf16[16,16,1536]{2,1,0:T(8,128)(2,1)S(1)} %columns.1), channel_id=1, replica_groups=mesh['slot'=16,'row'=16] {'row'}, dimensions={0} | all-to-all | bytes 1572864 | tf_op jit(solution)/shard_map/all_to_all | solution.py:232
  41.5 0.0 copy-done.1
  41.5 0.0 copy-start.4
  41.5 4.2 %rows.1 = bf16[16,16,1664]{2,1,0:T(8,128)(2,1)S(1)} custom-call(bf16[16,16,1536]{2,1,0:T(8,128)(2,1)S(1)} %all_to_all.10.x_ref, bf16[1536,1536]{1,0:T(8,128)(2,1)S(1)} %copy-done.1), custom_call_target="tpu_custom_call" | custom-call | tf_op jit(solution)/shard_map/rows/pallas_call | solution.py:246
  45.7 21.6 %all_to_all.11.z_ref = bf16[16,16,1664]{2,1,0:T(8,128)(2,1)S(1)} all-to-all(bf16[16,16,1664]{2,1,0:T(8,128)(2,1)S(1)} %rows.1), channel_id=1, replica_groups=mesh['slot'=16,'row'=16] {'slot'}, dimensions={0} | all-to-all | bytes 1703936 | tf_op jit(solution)/shard_map/all_to_all | solution.py:259
  67.3 0.0 copy-done.6
  67.4 0.0 copy-done.5
  67.4 3.7 %lags.1.own_ref = bf16[4,16,1664]{2,1,0:T(8,128)(2,1)S(1)} custom-call(s32[4]{0:T(128)S(1)} %copy-done.5, bf16[16,16,1664]{2,1,0:T(8,128)(2,1)S(1)} %all_to_all.11.z_ref, f32[16,1664]{1,0:T(8,128)S(1)} %jit_solution_.3.first_ref), custom_call_target="tpu_custom_call" | custom-call | tf_op jit(solution)/shard_map/lags/pallas_call | solution.py:262
  71.1 1.3 %collective-permute-start = (bf16[4,16,1664]{2,1,0:T(8,128)(2,1)S(1)}, bf16[4,16,1664]{2,1,0:T(8,128)(2,1)S(1)}, u32[]{:S(2)}, u32[]{:S(2)}) collective-permute-start(bf16[4,16,1664]{2,1,0:T(8,128)(2,1)S(1)} %lags.1.own_ref), channel_id=1, source_target_pairs={{0,255},{1,254},{2,253},{3,252},{4,251},{5,250},{6,249},{7,248},{8... | collective-permute-start | bytes 638984 | tf_op jit(solution)/shard_map/ppermute | solution.py:279
  72.4 16.4 %collective-permute-done.other_ref = bf16[4,16,1664]{2,1,0:T(8,128)(2,1)S(1)} collective-permute-done((bf16[4,16,1664]{2,1,0:T(8,128)(2,1)S(1)}, bf16[4,16,1664]{2,1,0:T(8,128)(2,1)S(1)}, u32[]{:S(2)}, u32[]{:S(2)}) %collective-permute-start) | collective-permute-done | bytes 213024 | tf_op jit(solution)/shard_map/ppermute | solution.py:279
  88.8 0.0 copy-done.4
  88.8 3.0 %place.1 = f32[2,4,3,88,88]{4,3,2,1,0:T(8,128)} custom-call(bf16[4,16,1664]{2,1,0:T(8,128)(2,1)S(1)} %lags.1.own_ref, bf16[4,16,1664]{2,1,0:T(8,128)(2,1)S(1)} %collective-permute-done.other_ref, bf16[256,256]{1,0:T(8,128)(2,1)S(1)} %copy-done.4), custom_call_target="tpu_custom_call" | custom-call | tf_op jit(solution)/shard_map/place/pallas_call | solution.py:281
  (1 shorter events, 0.0 us)
Async XLA Ops:
  0.0 2.6 %copy-start = (bf16[1408,2048]{1,0:T(8,128)(2,1)S(1)}, bf16[1408,2048]{1,0:T(8,128)(2,1)}, u32[]{:S(2)}) copy-start(bf16[1408,2048]{1,0:T(8,128)(2,1)} %constant.8.clone.table_ref) | copy-start | bytes 17301508
  2.6 1.4 %copy-start.2 = (s32[1,3,88,1408]{3,2,1,0:T(8,128)S(1)}, s32[1,3,88,1408]{3,2,1,0:T(8,128)}, u32[]{:S(2)}) copy-start(s32[1,3,88,1408]{3,2,1,0:T(8,128)} %mask_ref.1) | copy-start | bytes 4460548
  4.0 1.1 %copy-start.3 = (bf16[1,3,88,1408]{3,2,1,0:T(8,128)(2,1)S(1)}, bf16[1,3,88,1408]{3,2,1,0:T(8,128)(2,1)}, u32[]{:S(2)}) copy-start(bf16[1,3,88,1408]{3,2,1,0:T(8,128)(2,1)} %x_ref.1) | copy-start | bytes 2230276
  5.1 36.4 %copy-start.1 = (bf16[1536,1536]{1,0:T(8,128)(2,1)S(1)}, bf16[1536,1536]{1,0:T(8,128)(2,1)}, u32[]{:S(2)}) copy-start(bf16[1536,1536]{1,0:T(8,128)(2,1)} %constant.9.clone.table_ref) | copy-start | bytes 14155780
  8.8 58.5 %copy-start.6 = (f32[1664]{0:T(1024)S(1)}, f32[1664]{0:T(1024)}, u32[]{:S(2)}) copy-start(f32[1664]{0:T(1024)} %constant.10.clone) | copy-start | bytes 19972
  8.8 58.5 %copy-start.5 = (s32[4]{0:T(128)S(1)}, s32[4]{0:T(128)}, u32[]{:S(2)}) copy-start(s32[4]{0:T(128)} %lag_ref.1) | copy-start | bytes 52
  41.5 47.3 %copy-start.4 = (bf16[256,256]{1,0:T(8,128)(2,1)S(1)}, bf16[256,256]{1,0:T(8,128)(2,1)}, u32[]{:S(2)}) copy-start(bf16[256,256]{1,0:T(8,128)(2,1)} %constant.11.clone.spread_ref) | copy-start | bytes 393220
  71.1 17.7 %collective-permute-start = (bf16[4,16,1664]{2,1,0:T(8,128)(2,1)S(1)}, bf16[4,16,1664]{2,1,0:T(8,128)(2,1)S(1)}, u32[]{:S(2)}, u32[]{:S(2)}) collective-permute-start(bf16[4,16,1664]{2,1,0:T(8,128)(2,1)S(1)} %lags.1.own_ref), channel_id=1, source_target_pairs={{0,255},{1,254},{2,253},{3,252},{4,251},{5,250},{6,249},{7,248},{8... | collective-permute-start | bytes 638984 | tf_op jit(solution)/shard_map/ppermute | solution.py:279

commit v2 on v1

v2 whole, which is shorter than its diff:
```python
import functools
import math

import jax
import jax.numpy as jnp
import ml_dtypes
import numpy as np
from jax import lax
from jax.experimental import pallas as pl
from jax.experimental.pallas import tpu as pltpu
from jax.sharding import PartitionSpec as P

F32 = jnp.float32
BF16 = jnp.bfloat16
LANES = 128
GROUP = 16


def phase(numbers, length):
    return (numbers % length) * (2.0 * math.pi / length)


def column_table(length, parts, half, pitch, chunks):
    block = length // parts
    kx = (np.arange(parts)[:, None] * block + np.arange(half)[None, :]) % length
    angles = phase(np.arange(length)[:, None, None] * kx[None], length)
    table = np.zeros((length, parts, pitch))
    table[:, :, :half] = np.cos(angles)
    table[:, :, half : 2 * half] = -np.sin(angles)
    table = (table / math.sqrt(length)).reshape(length, chunks, parts // chunks * pitch)
    return np.ascontiguousarray(table.transpose(1, 0, 2)).astype(ml_dtypes.bfloat16)


def row_table(length, parts, rows_up, row_order):
    block = length // parts
    ky = np.arange(parts // 2)[:, None] * block + np.arange(block + 1)[None, :]
    angles = phase(ky[:, :, None] * row_order[None, None, :], length)
    table = np.zeros((parts // 2, 2, rows_up, row_order.size))
    table[:, 0, : block + 1] = np.cos(angles)
    table[:, 1, : block + 1] = np.sin(angles)
    return (table / math.sqrt(length)).reshape(-1, row_order.size).astype(ml_dtypes.bfloat16)


def lane_index(shape):
    return lax.broadcasted_iota(jnp.int32, shape, len(shape) - 1)


class Packed:
    def __init__(self, tiles):
        self.tiles = [jnp.zeros((GROUP, LANES), F32) for _ in range(tiles)]
        self.lane = lane_index((GROUP, LANES))

    def put(self, value, start, width):
        tile, shift = divmod(start, LANES)
        inside = self.lane >= shift
        if shift + width <= LANES:
            inside &= self.lane < shift + width
        else:
            after = self.lane < shift + width - LANES
            self.tiles[tile + 1] = jnp.where(after, value, self.tiles[tile + 1])
        self.tiles[tile] = jnp.where(inside, value, self.tiles[tile])


def turn(value, lanes):
    lanes %= LANES
    return pltpu.roll(value, lanes, 1) if lanes else value


def unpack(load, start, width, rows):
    lane = lane_index((rows, LANES))
    tile, shift = divmod(start, LANES)
    value = load(tile)
    if shift + width > LANES:
        value = jnp.where(lane >= shift, value, load(tile + 1))
    return jnp.where(lane < width, turn(value, -shift), 0.0)


def column_kernel(width, pitch, x_hbm, mask_hbm, table_hbm, out_ref, x, mask, table, left, x_sem, mask_sem, table_sem):
    channels, rows = x.shape[0], x.shape[1]
    chunks, parts = table.shape[0], out_ref.shape[0]
    x_copies = [pltpu.make_async_copy(x_hbm.at[0, c], x.at[c], x_sem.at[c]) for c in range(channels)]
    mask_copies = [pltpu.make_async_copy(mask_hbm.at[0, c], mask.at[c], mask_sem.at[c]) for c in range(channels)]
    table_copies = [pltpu.make_async_copy(table_hbm.at[n], table.at[n], table_sem.at[n]) for n in range(chunks)]
    for c in range(channels):
        mask_copies[c].start()
        x_copies[c].start()
    for copy in table_copies:
        copy.start()
    whole = rows // GROUP * GROUP
    tail = []
    for c in range(channels):
        mask_copies[c].wait()
        x_copies[c].wait()
        masked = x[c].astype(F32) * mask[c].astype(F32)
        left[c * whole : (c + 1) * whole] = masked[:whole].astype(BF16)
        tail.append(masked[whole:])
    spare = left.shape[0] - channels * rows
    if spare:
        tail.append(jnp.zeros((spare, left.shape[1]), F32))
    left[channels * whole :] = jnp.concatenate(tail, axis=0).astype(BF16)

    lane = lane_index((GROUP, LANES))
    for n in range(chunks):
        table_copies[n].wait()
        result = jnp.dot(left[...], table[n], preferred_element_type=F32)
        for k in range(parts // chunks):
            tile, shift = divmod(k * pitch, LANES)
            packed = Packed(out_ref.shape[2] // LANES)
            for g in range(left.shape[0] // GROUP):
                at = slice(g * GROUP, (g + 1) * GROUP)
                value = result[at, tile * LANES : (tile + 1) * LANES]
                if shift + width > LANES:
                    value = jnp.where(lane >= shift, value, result[at, (tile + 1) * LANES : (tile + 2) * LANES])
                packed.put(turn(value, g * width - shift), g * width, width)
            out_ref[n * (parts // chunks) + k] = jnp.concatenate(packed.tiles, axis=1).astype(BF16)


def split_rows(blocks, whole):
    groups = [v[a : a + GROUP] for v in blocks for a in range(0, whole, GROUP)]
    tail = [v[whole : whole + 8] for v in blocks]
    last = blocks[0][whole + 8 : whole + 16]
    for c in range(1, len(blocks)):
        last = last + pltpu.roll(blocks[c][whole + 8 : whole + 16], c, 0)
    tail.append(last)
    return groups + [jnp.concatenate(tail[i : i + 2], axis=0) for i in range(0, len(tail), 2)]


def join_rows(groups, channels, whole):
    per = whole // GROUP
    tail = []
    for value in groups[channels * per :]:
        tail += [value[:8], value[8:]]
    blocks = []
    for c in range(channels):
        last = pltpu.roll(tail[channels], 8 - c, 0) if c else tail[channels]
        blocks.append(jnp.concatenate(groups[c * per : (c + 1) * per] + [tail[c], last], axis=0))
    return blocks


def row_kernel(half, channels, rows_up, x_ref, table_ref, out_ref, right):
    width = 2 * half
    parts = x_ref.shape[0]
    depth = parts * GROUP
    steps = right.shape[0] // depth
    tiles = out_ref.shape[2] // LANES // 2

    def load(tile):
        return x_ref[:, :, tile * LANES : (tile + 1) * LANES].reshape(depth, LANES).astype(F32)

    row_in_group = lax.broadcasted_iota(jnp.int32, (depth, LANES), 0) % GROUP
    for c in range(channels):
        lanes = slice(c * LANES, (c + 1) * LANES)
        for a in range(steps - 1):
            value = unpack(load, (c * (steps - 1) + a) * width, width, depth)
            right[a * depth : (a + 1) * depth, lanes] = value.astype(BF16)
        value = unpack(load, (channels * (steps - 1) + c // 2) * width, width, depth)
        value = jnp.where((row_in_group >= GROUP // 2) == (c % 2 == 1), value, 0.0)
        right[(steps - 1) * depth :, lanes] = value.astype(BF16)

    for q in range(out_ref.shape[0] // 2):
        top = 2 * q * rows_up
        result = jnp.dot(table_ref[top : top + 2 * rows_up], right[...], preferred_element_type=F32)
        sides = []
        for at in (0, rows_up):
            blocks = [result[at : at + rows_up, c * LANES : (c + 1) * LANES] for c in range(channels)]
            sides.append(split_rows(blocks, rows_up - GROUP))
        out = [Packed(tiles) for _ in range(4)]
        for g, (even, odd) in enumerate(zip(*sides)):
            start = g * half
            real_even, real_odd = turn(even, start), turn(odd, start - half)
            imag_even, imag_odd = turn(even, start - half), turn(odd, start)
            out[0].put(real_even + real_odd, start, half)
            out[1].put(imag_even - imag_odd, start, half)
            out[2].put(real_even - real_odd, start, half)
            out[3].put(imag_even + imag_odd, start, half)
        for place, values in ((q, out[:2]), (out_ref.shape[0] - 1 - q, out[2:])):
            joined = jnp.concatenate(values[0].tiles + values[1].tiles, axis=1)
            out_ref[place] = joined.astype(BF16)


def lag_kernel(lag_ref, z_ref, out_ref, wide):
    slots, rows, lanes = z_ref.shape
    middle = lanes // 2
    for t in range(slots):
        wide[t] = z_ref[t].astype(F32)
    for entry in range(out_ref.shape[0]):
        lag = lag_ref[entry]

        def add(t, sums):
            early_real, early_imag = wide[t, :, :middle], wide[t, :, middle:]
            late_real, late_imag = wide[t + lag, :, :middle], wide[t + lag, :, middle:]
            return (
                sums[0] + (early_real * late_real + early_imag * late_imag),
                sums[1] + (early_imag * late_real - early_real * late_imag),
            )

        zero = jnp.zeros((rows, middle), F32)
        sums = lax.fori_loop(0, slots - lag, add, (zero, zero))
        scale = 1.0 / jnp.broadcast_to((slots - lag).astype(F32), (rows, LANES))
        for part in range(2):
            for at in range(0, middle, LANES):
                value = sums[part][:, at : at + LANES] * scale
                out_ref[entry, :, part * middle + at : part * middle + at + LANES] = value.astype(BF16)


def place_kernel(half, channels, rows_up, own_ref, other_ref, spread_ref, out_ref, both, spread):
    block = out_ref.shape[3]
    whole = rows_up - GROUP
    groups = channels * (rows_up // GROUP - 1) + (channels + 2) // 2
    middle = own_ref.shape[2] // 2
    at_row = lax.broadcasted_iota(jnp.int32, (rows_up, rows_up), 0)
    at_col = lax.broadcasted_iota(jnp.int32, (rows_up, rows_up), 1)
    back = lax.axis_index("slot") * 2 >= lax.axis_size("slot")
    source = jnp.where(back, block - at_row, at_row)
    order = (source == at_col).astype(F32).astype(BF16)
    entries = out_ref.shape[1]
    for part in range(2):
        for entry in range(entries):
            sides = []
            for ref in (own_ref, other_ref):

                def load(tile):
                    return ref[entry, :, tile * LANES : (tile + 1) * LANES].astype(F32)

                values = [unpack(load, part * middle + g * half, half, GROUP) for g in range(groups)]
                sides.append(join_rows(values, channels, whole))
            for c in range(channels):
                at = (part * entries + entry) * channels + c
                value = jnp.concatenate([sides[0][c], sides[1][c]], axis=1)
                both[at * rows_up : (at + 1) * rows_up] = value.astype(BF16)
    for part in range(2):
        for entry in range(entries):
            for c in range(channels):
                at = (part * entries + entry) * channels + c
                value = jnp.dot(both[at * rows_up : (at + 1) * rows_up], spread_ref[part], preferred_element_type=F32)
                spread[:, at * LANES : (at + 1) * LANES] = value.astype(BF16)
    for part in range(2):
        for entry in range(entries):
            for c in range(channels):
                at = (part * entries + entry) * channels + c
                value = jnp.dot(order, spread[:, at * LANES : (at + 1) * LANES], preferred_element_type=F32)
                out_ref[part, entry, c] = value[:block, :block]


def spread_table(block, half):
    table = np.zeros((2, 2 * LANES, LANES))
    for j in range(block):
        if j < half:
            table[:, j, j] = 1.0
        else:
            table[:, LANES + block - j, j] = (1.0, -1.0)
    return table.astype(ml_dtypes.bfloat16)


def up(value, unit):
    return -(-value // unit) * unit


def on_device(slots, parts, innovation, clear_mask, lag_list):
    _, channels, rows, cols = innovation.shape
    length = rows * parts
    block = cols // parts
    half = block // 2 + 1
    width = 2 * half
    entries = lag_list.shape[0]
    whole_vmem = pl.BlockSpec(memory_space=pltpu.VMEM)
    limit = pltpu.CompilerParams(vmem_limit_bytes=24 * 2**20)

    left_rows = up(channels * rows, GROUP)
    packed = up(left_rows // GROUP * width, LANES)
    pitch, chunks = 96, 2
    table = column_table(cols, parts, half, pitch, chunks)
    g = pl.pallas_call(
        functools.partial(column_kernel, width, pitch),
        in_specs=[pl.BlockSpec(memory_space=pl.ANY)] * 3,
        out_specs=whole_vmem,
        out_shape=jax.ShapeDtypeStruct((parts, GROUP, packed), BF16),
        scratch_shapes=[
            pltpu.VMEM(innovation.shape[1:], BF16),
            pltpu.VMEM(clear_mask.shape[1:], jnp.int32),
            pltpu.VMEM(table.shape, BF16),
            pltpu.VMEM((left_rows, cols), BF16),
            pltpu.SemaphoreType.DMA((channels,)),
            pltpu.SemaphoreType.DMA((channels,)),
            pltpu.SemaphoreType.DMA((chunks,)),
        ],
        compiler_params=pltpu.CompilerParams(vmem_limit_bytes=60 * 2**20),
        name="columns",
    )(innovation, clear_mask, jnp.asarray(table))
    g = lax.all_to_all(g, "row", 0, 0, tiled=True)

    whole = rows // GROUP
    order = [
        p * rows + (a * GROUP + b if a < whole else whole * GROUP + b % (GROUP // 2))
        for a in range(whole + 1)
        for p in range(parts)
        for b in range(GROUP)
    ]
    ky_block = length // slots
    rows_up = up(ky_block + 1, GROUP)
    table = row_table(length, slots, rows_up, np.array(order))
    packed = 2 * up((channels * (rows_up // GROUP - 1) + (channels + 2) // 2) * half, LANES)
    f = pl.pallas_call(
        functools.partial(row_kernel, half, channels, rows_up),
        in_specs=[whole_vmem] * 2,
        out_specs=whole_vmem,
        out_shape=jax.ShapeDtypeStruct((slots, GROUP, packed), BF16),
        scratch_shapes=[pltpu.VMEM((table.shape[1], channels * LANES), BF16)],
        compiler_params=limit,
        name="rows",
    )(g, jnp.asarray(table))
    f = lax.all_to_all(f, "slot", 0, 0, tiled=True)

    own = pl.pallas_call(
        lag_kernel,
        in_specs=[pl.BlockSpec(memory_space=pltpu.SMEM), whole_vmem],
        out_specs=whole_vmem,
        out_shape=jax.ShapeDtypeStruct((entries, GROUP, packed), BF16),
        scratch_shapes=[pltpu.VMEM((slots, GROUP, packed), F32)],
        compiler_params=limit,
        name="lags",
    )(lag_list, f)

    mirror = [
        (s * parts + p, (slots - 1 - s) * parts + parts - 1 - p) for s in range(slots) for p in range(parts)
    ]
    other = lax.ppermute(own, ("slot", "row"), mirror)

    planes = 2 * entries * channels
    return pl.pallas_call(
        functools.partial(place_kernel, half, channels, rows_up),
        in_specs=[whole_vmem] * 3,
        out_specs=whole_vmem,
        out_shape=jax.ShapeDtypeStruct((2, entries, channels, ky_block, block), F32),
        scratch_shapes=[pltpu.VMEM((planes * rows_up, 2 * LANES), BF16), pltpu.VMEM((rows_up, planes * LANES), BF16)],
        compiler_params=limit,
        name="place",
    )(own, other, jnp.asarray(spread_table(block, half)))


def solution(mesh):
    placed = (P("slot", None, "row", None), P("slot", None, "row", None), P())
    return jax.shard_map(
        functools.partial(on_device, mesh.shape["slot"], mesh.shape["row"]),
        mesh=mesh,
        in_specs=placed,
        out_specs=P(None, None, None, "slot", "row"),
        check_vma=False,
    )
```

time: 91.8 us -> 85 us (0.926)
  Pallas kernels: 14.5 us -> 11.6 us
  local copies, waits for them, and re-layouts: 5.16 us -> 2.34 us
    pallas_call x4, Pallas kernels: 14.5 us -> 11.6 us  [the longest x1 5.46 us: on_device(): pl.pallas_call(functools.partial(column_kernel, width, pitch), in_specs=[...]
    unnamed x14 -> x6, local copies, waits for them, and re-layouts: 5.15 us -> 2.34 us
where the time goes in v2:
time: 85 us; the launch traced here: 84.7 us
  blocking collectives  53.8 us (63%)
  waiting for transfers between devices  15.6 us (18%)
  Pallas kernels  11.6 us (14%)
  local copies, waits for them, and re-layouts  2.34 us (3%)
  starting transfers between devices  1.35 us (2%)
    all_to_all x1, blocking collectives, on_device(): g = lax.all_to_all(g, 'row', 0, 0, tiled=True)  32.9 us
    all_to_all x1, blocking collectives, on_device(): f = lax.all_to_all(f, 'slot', 0, 0, tiled=True)  20.9 us
    ppermute x1, waiting for transfers between devices, on_device(): other = lax.ppermute(own, ('slot', 'row'), mirror)  15.6 us
    pallas_call x1, Pallas kernels, on_device(): pl.pallas_call(functools.partial(column_kernel, width, pitch), in_specs=[...  5.46 us
    pallas_call x1, Pallas kernels, on_device(): pl.pallas_call(functools.partial(row_kernel, half, channels, rows_up), in...  3.2 us
    unnamed x6, local copies, waits for them, and re-layouts  2.34 us
  transfers between devices with their start and end apart: 1, of which 1 were waited for; matrix products, arithmetic and copies ran while one was open for 0% of the time, Pallas kernels for 0%

profile of v2, /device:TPU:1, one launch (start us, length us, event | category | flops | bytes accessed | tf_op | source)
XLA Modules:
  0.0 84.7 jit_solution(12965175518737950727)
XLA Ops:
  0.0 5.5 %columns.1 = bf16[16,16,1536]{2,1,0:T(8,128)(2,1)} custom-call(bf16[1,3,88,1408]{3,2,1,0:T(8,128)(2,1)} %x_hbm.1, s32[1,3,88,1408]{3,2,1,0:T(8,128)} %mask_hbm.1, bf16[2,1408,768]{2,1,0:T(8,128)(2,1)} %constant.6.clone.table_hbm), custom_call_target="tpu_custom_call" | custom-call | tf_op jit(solution)/shard_map/columns/pallas_call | solution.py:273
  5.5 32.9 %all_to_all.10.x_ref = bf16[16,16,1536]{2,1,0:T(8,128)(2,1)S(1)} all-to-all(bf16[16,16,1536]{2,1,0:T(8,128)(2,1)} %columns.1), channel_id=1, replica_groups=mesh['slot'=16,'row'=16] {'row'}, dimensions={0} | all-to-all | bytes 1572864 | tf_op jit(solution)/shard_map/all_to_all | solution.py:290
  38.4 0.0 copy-start
  38.4 2.3 %copy-done = bf16[1536,1536]{1,0:T(8,128)(2,1)S(1)} copy-done((bf16[1536,1536]{1,0:T(8,128)(2,1)S(1)}, bf16[1536,1536]{1,0:T(8,128)(2,1)}, u32[]{:S(2)}) %copy-start) | copy-done | bytes 4718616
  40.7 0.0 copy-start.2
  40.7 0.0 copy-start.1
  40.7 3.2 %rows.1 = bf16[16,16,1536]{2,1,0:T(8,128)(2,1)S(1)} custom-call(bf16[16,16,1536]{2,1,0:T(8,128)(2,1)S(1)} %all_to_all.10.x_ref, bf16[1536,1536]{1,0:T(8,128)(2,1)S(1)} %copy-done), custom_call_target="tpu_custom_call" | custom-call | tf_op jit(solution)/shard_map/rows/pallas_call | solution.py:303
  43.9 20.9 %all_to_all.11.z_ref = bf16[16,16,1536]{2,1,0:T(8,128)(2,1)S(1)} all-to-all(bf16[16,16,1536]{2,1,0:T(8,128)(2,1)S(1)} %rows.1), channel_id=1, replica_groups=mesh['slot'=16,'row'=16] {'slot'}, dimensions={0} | all-to-all | bytes 1572864 | tf_op jit(solution)/shard_map/all_to_all | solution.py:312
  64.8 0.0 copy-done.2
  64.8 1.2 %lags.1.own_ref = bf16[4,16,1536]{2,1,0:T(8,128)(2,1)S(1)} custom-call(s32[4]{0:T(128)S(1)} %copy-done.2, bf16[16,16,1536]{2,1,0:T(8,128)(2,1)S(1)} %all_to_all.11.z_ref), custom_call_target="tpu_custom_call" | custom-call | tf_op jit(solution)/shard_map/lags/pallas_call | solution.py:314
  66.1 1.4 %collective-permute-start = (bf16[4,16,1536]{2,1,0:T(8,128)(2,1)S(1)}, bf16[4,16,1536]{2,1,0:T(8,128)(2,1)S(1)}, u32[]{:S(2)}, u32[]{:S(2)}) collective-permute-start(bf16[4,16,1536]{2,1,0:T(8,128)(2,1)S(1)} %lags.1.own_ref), channel_id=1, source_target_pairs={{0,255},{1,254},{2,253},{3,252},{4,251},{5,250},{6,249},{7,248},{8... | collective-permute-start | bytes 589832 | tf_op jit(solution)/shard_map/ppermute | solution.py:327
  67.4 15.6 %collective-permute-done.other_ref = bf16[4,16,1536]{2,1,0:T(8,128)(2,1)S(1)} collective-permute-done((bf16[4,16,1536]{2,1,0:T(8,128)(2,1)S(1)}, bf16[4,16,1536]{2,1,0:T(8,128)(2,1)S(1)}, u32[]{:S(2)}, u32[]{:S(2)}) %collective-permute-start) | collective-permute-done | bytes 196640 | tf_op jit(solution)/shard_map/ppermute | solution.py:327
  83.0 0.0 copy-done.1
  83.0 1.7 %place.1 = f32[2,4,3,88,88]{4,3,2,1,0:T(8,128)} custom-call(bf16[4,16,1536]{2,1,0:T(8,128)(2,1)S(1)} %lags.1.own_ref, bf16[4,16,1536]{2,1,0:T(8,128)(2,1)S(1)} %collective-permute-done.other_ref, bf16[2,256,128]{2,1,0:T(8,128)(2,1)S(1)} %copy-done.1), custom_call_target="tpu_custom_call" | custom-call | tf_op jit(solution)/shard_map/place/pallas_call | solution.py:330
Async XLA Ops:
  38.4 2.3 %copy-start = (bf16[1536,1536]{1,0:T(8,128)(2,1)S(1)}, bf16[1536,1536]{1,0:T(8,128)(2,1)}, u32[]{:S(2)}) copy-start(bf16[1536,1536]{1,0:T(8,128)(2,1)} %constant.7.clone.table_ref) | copy-start | bytes 14155780
  40.7 24.1 %copy-start.2 = (s32[4]{0:T(128)S(1)}, s32[4]{0:T(128)}, u32[]{:S(2)}) copy-start(s32[4]{0:T(128)} %lag_ref.1) | copy-start | bytes 52
  40.7 42.3 %copy-start.1 = (bf16[2,256,128]{2,1,0:T(8,128)(2,1)S(1)}, bf16[2,256,128]{2,1,0:T(8,128)(2,1)}, u32[]{:S(2)}) copy-start(bf16[2,256,128]{2,1,0:T(8,128)(2,1)} %constant.8.clone.spread_ref) | copy-start | bytes 393220
  66.1 16.9 %collective-permute-start = (bf16[4,16,1536]{2,1,0:T(8,128)(2,1)S(1)}, bf16[4,16,1536]{2,1,0:T(8,128)(2,1)S(1)}, u32[]{:S(2)}, u32[]{:S(2)}) collective-permute-start(bf16[4,16,1536]{2,1,0:T(8,128)(2,1)S(1)} %lags.1.own_ref), channel_id=1, source_target_pairs={{0,255},{1,254},{2,253},{3,252},{4,251},{5,250},{6,249},{7,248},{8... | collective-permute-start | bytes 589832 | tf_op jit(solution)/shard_map/ppermute | solution.py:327

commit v3 on v2

--- a/solution.py
+++ b/solution.py
@@ -72,7 +72,7 @@
     value = load(tile)
     if shift + width > LANES:
         value = jnp.where(lane >= shift, value, load(tile + 1))
-    return jnp.where(lane < width, turn(value, -shift), 0.0)
+    return jnp.where(lane < width, turn(value, -shift), jnp.zeros((), BF16))
 
 
 def column_kernel(width, pitch, x_hbm, mask_hbm, table_hbm, out_ref, x, mask, table, left, x_sem, mask_sem, table_sem):
@@ -145,17 +145,17 @@
     tiles = out_ref.shape[2] // LANES // 2
 
     def load(tile):
-        return x_ref[:, :, tile * LANES : (tile + 1) * LANES].reshape(depth, LANES).astype(F32)
+        return x_ref[:, :, tile * LANES : (tile + 1) * LANES].reshape(depth, LANES)
 
     row_in_group = lax.broadcasted_iota(jnp.int32, (depth, LANES), 0) % GROUP
     for c in range(channels):
         lanes = slice(c * LANES, (c + 1) * LANES)
         for a in range(steps - 1):
             value = unpack(load, (c * (steps - 1) + a) * width, width, depth)
-            right[a * depth : (a + 1) * depth, lanes] = value.astype(BF16)
+            right[a * depth : (a + 1) * depth, lanes] = value
         value = unpack(load, (channels * (steps - 1) + c // 2) * width, width, depth)
-        value = jnp.where((row_in_group >= GROUP // 2) == (c % 2 == 1), value, 0.0)
-        right[(steps - 1) * depth :, lanes] = value.astype(BF16)
+        value = jnp.where((row_in_group >= GROUP // 2) == (c % 2 == 1), value, jnp.zeros((), BF16))
+        right[(steps - 1) * depth :, lanes] = value
 
     for q in range(out_ref.shape[0] // 2):
         top = 2 * q * rows_up
@@ -220,9 +220,9 @@
             for ref in (own_ref, other_ref):
 
                 def load(tile):
-                    return ref[entry, :, tile * LANES : (tile + 1) * LANES].astype(F32)
-
-                values = [unpack(load, part * middle + g * half, half, GROUP) for g in range(groups)]
+                    return ref[entry, :, tile * LANES : (tile + 1) * LANES]
+
+                values = [unpack(load, part * middle + g * half, half, GROUP).astype(F32) for g in range(groups)]
                 sides.append(join_rows(values, channels, whole))
             for c in range(channels):
                 at = (part * entries + entry) * channels + c
@@ -284,7 +284,7 @@
             pltpu.SemaphoreType.DMA((channels,)),
             pltpu.SemaphoreType.DMA((chunks,)),
         ],
-        compiler_params=pltpu.CompilerParams(vmem_limit_bytes=60 * 2**20),
+        compiler_params=pltpu.CompilerParams(vmem_limit_bytes=57 * 2**20),
         name="columns",
     )(innovation, clear_mask, jnp.asarray(table))
     g = lax.all_to_all(g, "row", 0, 0, tiled=True)

time: 85 us -> 82.9 us (0.975)
  local copies, waits for them, and re-layouts: 2.34 us -> 0.02 us
    unnamed x6 -> x8, local copies, waits for them, and re-layouts: 2.34 us -> 0.02 us
where the time goes in v3:
time: 82.9 us; the launch traced here: 82.8 us
  blocking collectives  53.8 us (65%)
  waiting for transfers between devices  15.6 us (19%)
  Pallas kernels  12 us (14%)
  starting transfers between devices  1.35 us (2%)
    all_to_all x1, blocking collectives, on_device(): g = lax.all_to_all(g, 'row', 0, 0, tiled=True)  32.9 us
    all_to_all x1, blocking collectives, on_device(): f = lax.all_to_all(f, 'slot', 0, 0, tiled=True)  20.9 us
    ppermute x1, waiting for transfers between devices, on_device(): other = lax.ppermute(own, ('slot', 'row'), mirror)  15.6 us
    pallas_call x1, Pallas kernels, on_device(): pl.pallas_call(functools.partial(column_kernel, width, pitch), in_specs=[...  5.61 us
    pallas_call x1, Pallas kernels, on_device(): pl.pallas_call(functools.partial(row_kernel, half, channels, rows_up), in...  2.97 us
    pallas_call x1, Pallas kernels, on_device(): pl.pallas_call(lag_kernel, in_specs=[pl.BlockSpec(memory_space=pltpu.SMEM...  1.79 us
    pallas_call x1, Pallas kernels, on_device(): pl.pallas_call(functools.partial(place_kernel, half, channels, rows_up),...  1.66 us
  transfers between devices with their start and end apart: 1, of which 1 were waited for; matrix products, arithmetic and copies ran while one was open for 0% of the time, Pallas kernels for 0%

profile of v3, /device:TPU:1, one launch (start us, length us, event | category | flops | bytes accessed | tf_op | source)
XLA Modules:
  0.0 82.8 jit_solution(14596327080602330142)
XLA Ops:
  0.0 0.0 slice-start
  0.0 0.0 slice-start.1
  0.0 5.6 %columns.1 = bf16[16,16,1536]{2,1,0:T(8,128)(2,1)} custom-call(bf16[1,3,88,1408]{3,2,1,0:T(8,128)(2,1)} %x_hbm.1, s32[1,3,88,1408]{3,2,1,0:T(8,128)} %mask_hbm.1, bf16[2,1408,768]{2,1,0:T(8,128)(2,1)} %constant.6.clone.table_hbm), custom_call_target="tpu_custom_call" | custom-call | tf_op jit(solution)/shard_map/columns/pallas_call | solution.py:273
  5.6 32.9 %all_to_all.10.x_ref = bf16[16,16,1536]{2,1,0:T(8,128)(2,1)S(1)} all-to-all(bf16[16,16,1536]{2,1,0:T(8,128)(2,1)} %columns.1), channel_id=1, replica_groups=mesh['slot'=16,'row'=16] {'row'}, dimensions={0} | all-to-all | bytes 1572864 | tf_op jit(solution)/shard_map/all_to_all | solution.py:290
  38.5 0.0 slice-done
  38.5 0.0 slice-done.1
  38.5 0.0 copy-start.1
  38.6 0.0 copy-start
  38.6 3.0 %rows.1 = bf16[16,16,1536]{2,1,0:T(8,128)(2,1)S(1)} custom-call(bf16[16,16,1536]{2,1,0:T(8,128)(2,1)S(1)} %all_to_all.10.x_ref, bf16[1536,1536]{1,0:T(8,128)(2,1)S(1)} %bitcast.1), custom_call_target="tpu_custom_call" | custom-call | tf_op jit(solution)/shard_map/rows/pallas_call | solution.py:303
  41.5 20.9 %all_to_all.11.z_ref = bf16[16,16,1536]{2,1,0:T(8,128)(2,1)S(1)} all-to-all(bf16[16,16,1536]{2,1,0:T(8,128)(2,1)S(1)} %rows.1), channel_id=1, replica_groups=mesh['slot'=16,'row'=16] {'slot'}, dimensions={0} | all-to-all | bytes 1572864 | tf_op jit(solution)/shard_map/all_to_all | solution.py:312
  62.4 0.0 copy-done.1
  62.4 1.8 %lags.1.own_ref = bf16[4,16,1536]{2,1,0:T(8,128)(2,1)S(1)} custom-call(s32[4]{0:T(128)S(1)} %copy-done.1, bf16[16,16,1536]{2,1,0:T(8,128)(2,1)S(1)} %all_to_all.11.z_ref), custom_call_target="tpu_custom_call" | custom-call | tf_op jit(solution)/shard_map/lags/pallas_call | solution.py:314
  64.2 1.3 %collective-permute-start = (bf16[4,16,1536]{2,1,0:T(8,128)(2,1)S(1)}, bf16[4,16,1536]{2,1,0:T(8,128)(2,1)S(1)}, u32[]{:S(2)}, u32[]{:S(2)}) collective-permute-start(bf16[4,16,1536]{2,1,0:T(8,128)(2,1)S(1)} %lags.1.own_ref), channel_id=1, source_target_pairs={{0,255},{1,254},{2,253},{3,252},{4,251},{5,250},{6,249},{7,248},{8... | collective-permute-start | bytes 589832 | tf_op jit(solution)/shard_map/ppermute | solution.py:327
  65.6 15.6 %collective-permute-done.other_ref = bf16[4,16,1536]{2,1,0:T(8,128)(2,1)S(1)} collective-permute-done((bf16[4,16,1536]{2,1,0:T(8,128)(2,1)S(1)}, bf16[4,16,1536]{2,1,0:T(8,128)(2,1)S(1)}, u32[]{:S(2)}, u32[]{:S(2)}) %collective-permute-start) | collective-permute-done | bytes 196640 | tf_op jit(solution)/shard_map/ppermute | solution.py:327
  81.2 0.0 copy-done
  81.2 1.7 %place.1 = f32[2,4,3,88,88]{4,3,2,1,0:T(8,128)} custom-call(bf16[4,16,1536]{2,1,0:T(8,128)(2,1)S(1)} %lags.1.own_ref, bf16[4,16,1536]{2,1,0:T(8,128)(2,1)S(1)} %collective-permute-done.other_ref, bf16[2,256,128]{2,1,0:T(8,128)(2,1)S(1)} %copy-done), custom_call_target="tpu_custom_call" | custom-call | tf_op jit(solution)/shard_map/place/pallas_call | solution.py:330
  (1 shorter events, 0.0 us)
Async XLA Ops:
  0.0 38.5 %slice-start = ((s8[4718592]{0:T(1024)(128)(4,1)}), s8[4194304]{0:T(1024)(128)(4,1)S(1)}, s32[]{:S(2)}) async-start(s8[4718592]{0:T(1024)(128)(4,1)} %bitcast), calls=%async_computation.2 | async-start | bytes 8388608
  0.0 38.5 %slice-start.1 = ((s8[4718592]{0:T(1024)(128)(4,1)}), s8[524288]{0:T(1024)(128)(4,1)S(1)}, s32[]{:S(2)}) async-start(s8[4718592]{0:T(1024)(128)(4,1)} %bitcast), calls=%async_computation.3 | async-start | bytes 1048576
  38.5 23.9 %copy-start.1 = (s32[4]{0:T(128)S(1)}, s32[4]{0:T(128)}, u32[]{:S(2)}) copy-start(s32[4]{0:T(128)} %lag_ref.1) | copy-start | bytes 52
  38.6 42.6 %copy-start = (bf16[2,256,128]{2,1,0:T(8,128)(2,1)S(1)}, bf16[2,256,128]{2,1,0:T(8,128)(2,1)}, u32[]{:S(2)}) copy-start(bf16[2,256,128]{2,1,0:T(8,128)(2,1)} %constant.8.clone.spread_ref) | copy-start | bytes 393220
  64.2 16.9 %collective-permute-start = (bf16[4,16,1536]{2,1,0:T(8,128)(2,1)S(1)}, bf16[4,16,1536]{2,1,0:T(8,128)(2,1)S(1)}, u32[]{:S(2)}, u32[]{:S(2)}) collective-permute-start(bf16[4,16,1536]{2,1,0:T(8,128)(2,1)S(1)} %lags.1.own_ref), channel_id=1, source_target_pairs={{0,255},{1,254},{2,253},{3,252},{4,251},{5,250},{6,249},{7,248},{8... | collective-permute-start | bytes 589832 | tf_op jit(solution)/shard_map/ppermute | solution.py:327

commit v4 on v3

--- a/solution.py
+++ b/solution.py
@@ -14,28 +14,28 @@
 BF16 = jnp.bfloat16
 LANES = 128
 GROUP = 16
+CUT = 768
 
 
 def phase(numbers, length):
     return (numbers % length) * (2.0 * math.pi / length)
 
 
-def column_table(length, parts, half, pitch, chunks):
+def column_table(length, parts, half, pitch):
     block = length // parts
-    kx = (np.arange(parts)[:, None] * block + np.arange(half)[None, :]) % length
+    kx = np.arange(parts // 2)[:, None] * block + np.arange(half)[None, :]
     angles = phase(np.arange(length)[:, None, None] * kx[None], length)
-    table = np.zeros((length, parts, pitch))
+    table = np.zeros((length, parts // 2, pitch))
     table[:, :, :half] = np.cos(angles)
     table[:, :, half : 2 * half] = -np.sin(angles)
-    table = (table / math.sqrt(length)).reshape(length, chunks, parts // chunks * pitch)
-    return np.ascontiguousarray(table.transpose(1, 0, 2)).astype(ml_dtypes.bfloat16)
+    return (table / math.sqrt(length)).reshape(length, parts // 2 * pitch).astype(ml_dtypes.bfloat16)
 
 
 def row_table(length, parts, rows_up, row_order):
     block = length // parts
-    ky = np.arange(parts // 2)[:, None] * block + np.arange(block + 1)[None, :]
+    ky = np.arange(parts // 4)[:, None] * block + np.arange(block + 1)[None, :]
     angles = phase(ky[:, :, None] * row_order[None, None, :], length)
-    table = np.zeros((parts // 2, 2, rows_up, row_order.size))
+    table = np.zeros((parts // 4, 2, rows_up, row_order.size))
     table[:, 0, : block + 1] = np.cos(angles)
     table[:, 1, : block + 1] = np.sin(angles)
     return (table / math.sqrt(length)).reshape(-1, row_order.size).astype(ml_dtypes.bfloat16)
@@ -75,12 +75,15 @@
     return jnp.where(lane < width, turn(value, -shift), jnp.zeros((), BF16))
 
 
-def column_kernel(width, pitch, x_hbm, mask_hbm, table_hbm, out_ref, x, mask, table, left, x_sem, mask_sem, table_sem):
+def column_kernel(
+    width, pitch, x_hbm, mask_hbm, table_hbm, out_ref, x, mask, table, left, result, x_sem, mask_sem, table_sem
+):
     channels, rows = x.shape[0], x.shape[1]
-    chunks, parts = table.shape[0], out_ref.shape[0]
+    parts, used = out_ref.shape[0], left.shape[0] // 2
     x_copies = [pltpu.make_async_copy(x_hbm.at[0, c], x.at[c], x_sem.at[c]) for c in range(channels)]
     mask_copies = [pltpu.make_async_copy(mask_hbm.at[0, c], mask.at[c], mask_sem.at[c]) for c in range(channels)]
-    table_copies = [pltpu.make_async_copy(table_hbm.at[n], table.at[n], table_sem.at[n]) for n in range(chunks)]
+    cuts = [slice(0, CUT), slice(CUT, table.shape[0])]
+    table_copies = [pltpu.make_async_copy(table_hbm.at[k], table.at[k], table_sem.at[n]) for n, k in enumerate(cuts)]
     for c in range(channels):
         mask_copies[c].start()
         x_copies[c].start()
@@ -88,31 +91,40 @@
         copy.start()
     whole = rows // GROUP * GROUP
     tail = []
+
+    def store(at, value):
+        odd = lane_index(value.shape) % 2 == 1
+        left[at : at + value.shape[0]] = value.astype(BF16)
+        left[used + at : used + at + value.shape[0]] = jnp.where(odd, -value, value).astype(BF16)
+
     for c in range(channels):
         mask_copies[c].wait()
         x_copies[c].wait()
         masked = x[c].astype(F32) * mask[c].astype(F32)
-        left[c * whole : (c + 1) * whole] = masked[:whole].astype(BF16)
+        store(c * whole, masked[:whole])
         tail.append(masked[whole:])
-    spare = left.shape[0] - channels * rows
+    spare = used - channels * rows
     if spare:
         tail.append(jnp.zeros((spare, left.shape[1]), F32))
-    left[channels * whole :] = jnp.concatenate(tail, axis=0).astype(BF16)
+    store(channels * whole, jnp.concatenate(tail, axis=0))
+
+    for n, k in enumerate(cuts):
+        table_copies[n].wait()
+        value = jnp.dot(left[:, k], table[k], preferred_element_type=F32)
+        result[...] = result[...] + value if n else value
 
     lane = lane_index((GROUP, LANES))
-    for n in range(chunks):
-        table_copies[n].wait()
-        result = jnp.dot(left[...], table[n], preferred_element_type=F32)
-        for k in range(parts // chunks):
-            tile, shift = divmod(k * pitch, LANES)
+    for k in range(parts // 2):
+        tile, shift = divmod(k * pitch, LANES)
+        for side in range(2):
             packed = Packed(out_ref.shape[2] // LANES)
-            for g in range(left.shape[0] // GROUP):
-                at = slice(g * GROUP, (g + 1) * GROUP)
+            for g in range(used // GROUP):
+                at = slice(side * used + g * GROUP, side * used + (g + 1) * GROUP)
                 value = result[at, tile * LANES : (tile + 1) * LANES]
                 if shift + width > LANES:
                     value = jnp.where(lane >= shift, value, result[at, (tile + 1) * LANES : (tile + 2) * LANES])
                 packed.put(turn(value, g * width - shift), g * width, width)
-            out_ref[n * (parts // chunks) + k] = jnp.concatenate(packed.tiles, axis=1).astype(BF16)
+            out_ref[side * (parts // 2) + k] = jnp.concatenate(packed.tiles, axis=1).astype(BF16)
 
 
 def split_rows(blocks, whole):
@@ -148,42 +160,65 @@
         return x_ref[:, :, tile * LANES : (tile + 1) * LANES].reshape(depth, LANES)
 
     row_in_group = lax.broadcasted_iota(jnp.int32, (depth, LANES), 0) % GROUP
+    odd_row = row_in_group % 2 == 1
+
+    def store(a, c, value):
+        at = slice(a * depth, (a + 1) * depth)
+        right[at, c * LANES : (c + 1) * LANES] = value
+        right[at, (channels + c) * LANES : (channels + c + 1) * LANES] = jnp.where(odd_row, -value, value)
+
     for c in range(channels):
-        lanes = slice(c * LANES, (c + 1) * LANES)
         for a in range(steps - 1):
-            value = unpack(load, (c * (steps - 1) + a) * width, width, depth)
-            right[a * depth : (a + 1) * depth, lanes] = value
+            store(a, c, unpack(load, (c * (steps - 1) + a) * width, width, depth))
         value = unpack(load, (channels * (steps - 1) + c // 2) * width, width, depth)
         value = jnp.where((row_in_group >= GROUP // 2) == (c % 2 == 1), value, jnp.zeros((), BF16))
-        right[(steps - 1) * depth :, lanes] = value
-
-    for q in range(out_ref.shape[0] // 2):
+        store(steps - 1, c, value)
+
+    slots = out_ref.shape[0]
+    for q in range(slots // 4):
         top = 2 * q * rows_up
         result = jnp.dot(table_ref[top : top + 2 * rows_up], right[...], preferred_element_type=F32)
-        sides = []
-        for at in (0, rows_up):
-            blocks = [result[at : at + rows_up, c * LANES : (c + 1) * LANES] for c in range(channels)]
-            sides.append(split_rows(blocks, rows_up - GROUP))
-        out = [Packed(tiles) for _ in range(4)]
-        for g, (even, odd) in enumerate(zip(*sides)):
-            start = g * half
-            real_even, real_odd = turn(even, start), turn(odd, start - half)
-            imag_even, imag_odd = turn(even, start - half), turn(odd, start)
-            out[0].put(real_even + real_odd, start, half)
-            out[1].put(imag_even - imag_odd, start, half)
-            out[2].put(real_even - real_odd, start, half)
-            out[3].put(imag_even + imag_odd, start, half)
-        for place, values in ((q, out[:2]), (out_ref.shape[0] - 1 - q, out[2:])):
-            joined = jnp.concatenate(values[0].tiles + values[1].tiles, axis=1)
-            out_ref[place] = joined.astype(BF16)
-
-
-def lag_kernel(lag_ref, z_ref, out_ref, wide):
+        for shifted in range(2):
+            sides = []
+            for at in (0, rows_up):
+                lanes = [slice((shifted * channels + c) * LANES, (shifted * channels + c + 1) * LANES) for c in range(channels)]
+                sides.append(split_rows([result[at : at + rows_up, l] for l in lanes], rows_up - GROUP))
+            out = [Packed(tiles) for _ in range(4)]
+            for g, (even, odd) in enumerate(zip(*sides)):
+                start = g * half
+                real_even, real_odd = turn(even, start), turn(odd, start - half)
+                imag_even, imag_odd = turn(even, start - half), turn(odd, start)
+                out[0].put(real_even + real_odd, start, half)
+                out[1].put(imag_even - imag_odd, start, half)
+                out[2].put(real_even - real_odd, start, half)
+                out[3].put(imag_even + imag_odd, start, half)
+            place = q + shifted * (slots // 2)
+            for at, values in ((place, out[:2]), (slots - 1 - place, out[2:])):
+                joined = jnp.concatenate(values[0].tiles + values[1].tiles, axis=1)
+                out_ref[at] = joined.astype(BF16)
+
+
+def zero_entry(lag_ref, entries):
+    found = entries - 1
+    for entry in reversed(range(entries - 1)):
+        found = jnp.where(lag_ref[entry] == 0, entry, found)
+    return found
+
+
+def lag_kernel(lag_hbm, z_ref, own_ref, sent_ref, pick_ref, wide, lag_ref, lag_sem):
     slots, rows, lanes = z_ref.shape
     middle = lanes // 2
+    entries = own_ref.shape[0] // 2
+    lag_copy = pltpu.make_async_copy(lag_hbm, lag_ref, lag_sem)
+    lag_copy.start()
     for t in range(slots):
         wide[t] = z_ref[t].astype(F32)
-    for entry in range(out_ref.shape[0]):
+    lag_copy.wait()
+    still = zero_entry(lag_ref, entries)
+    for entry in range(entries):
+        for earlier, here in enumerate((entry < still, entry > still)):
+            pick_ref[entry, earlier] = jnp.broadcast_to(jnp.where(here, 1.0, 0.0), pick_ref.shape[2:]).astype(BF16)
+    for entry in range(entries):
         lag = lag_ref[entry]
 
         def add(t, sums):
@@ -197,32 +232,47 @@
         zero = jnp.zeros((rows, middle), F32)
         sums = lax.fori_loop(0, slots - lag, add, (zero, zero))
         scale = 1.0 / jnp.broadcast_to((slots - lag).astype(F32), (rows, LANES))
-        for part in range(2):
-            for at in range(0, middle, LANES):
-                value = sums[part][:, at : at + LANES] * scale
-                out_ref[entry, :, part * middle + at : part * middle + at + LANES] = value.astype(BF16)
-
-
-def place_kernel(half, channels, rows_up, own_ref, other_ref, spread_ref, out_ref, both, spread):
+        place = entries + entry - jnp.where(entry > still, 1, 0)
+        for at in range(0, middle, LANES):
+            value = (sums[0][:, at : at + LANES] * scale).astype(BF16)
+            own_ref[entry, :, at : at + LANES] = value
+            sent_ref[entry, :, at : at + LANES] = value
+            own_ref[entries + entry, :, at : at + LANES] = (sums[1][:, at : at + LANES] * scale).astype(BF16)
+
+        @pl.when(entry != still)
+        def _():
+            sent_ref[place] = own_ref[entries + entry]
+
+
+def place_kernel(half, channels, rows_up, own_ref, other_ref, pick_ref, spread_ref, out_ref, imag, both, spread):
     block = out_ref.shape[3]
     whole = rows_up - GROUP
     groups = channels * (rows_up // GROUP - 1) + (channels + 2) // 2
-    middle = own_ref.shape[2] // 2
     at_row = lax.broadcasted_iota(jnp.int32, (rows_up, rows_up), 0)
     at_col = lax.broadcasted_iota(jnp.int32, (rows_up, rows_up), 1)
-    back = lax.axis_index("slot") * 2 >= lax.axis_size("slot")
+    back = lax.axis_index("slot") // (lax.axis_size("slot") // 4) % 2 == 1
     source = jnp.where(back, block - at_row, at_row)
     order = (source == at_col).astype(F32).astype(BF16)
     entries = out_ref.shape[1]
+    for entry in range(entries):
+        for at in range(0, imag.shape[2], LANES):
+            value = jnp.zeros((GROUP, LANES), BF16)
+            if entry < entries - 1:
+                value += pick_ref[entry, 0] * other_ref[entries + entry, :, at : at + LANES]
+            if entry > 0:
+                value += pick_ref[entry, 1] * other_ref[entries + entry - 1, :, at : at + LANES]
+            imag[entry, :, at : at + LANES] = value
     for part in range(2):
         for entry in range(entries):
             sides = []
-            for ref in (own_ref, other_ref):
+            for mirrored in range(2):
+
+                ref, first = ((own_ref, part * entries), (imag if part else other_ref, 0))[mirrored]
 
                 def load(tile):
-                    return ref[entry, :, tile * LANES : (tile + 1) * LANES]
-
-                values = [unpack(load, part * middle + g * half, half, GROUP).astype(F32) for g in range(groups)]
+                    return ref[first + entry, :, tile * LANES : (tile + 1) * LANES]
+
+                values = [unpack(load, g * half, half, GROUP).astype(F32) for g in range(groups)]
                 sides.append(join_rows(values, channels, whole))
             for c in range(channels):
                 at = (part * entries + entry) * channels + c
@@ -268,8 +318,8 @@
 
     left_rows = up(channels * rows, GROUP)
     packed = up(left_rows // GROUP * width, LANES)
-    pitch, chunks = 96, 2
-    table = column_table(cols, parts, half, pitch, chunks)
+    pitch = 96
+    table = column_table(cols, parts, half, pitch)
     g = pl.pallas_call(
         functools.partial(column_kernel, width, pitch),
         in_specs=[pl.BlockSpec(memory_space=pl.ANY)] * 3,
@@ -279,10 +329,11 @@
             pltpu.VMEM(innovation.shape[1:], BF16),
             pltpu.VMEM(clear_mask.shape[1:], jnp.int32),
             pltpu.VMEM(table.shape, BF16),
-            pltpu.VMEM((left_rows, cols), BF16),
+            pltpu.VMEM((2 * left_rows, cols), BF16),
+            pltpu.VMEM((2 * left_rows, parts // 2 * pitch), F32),
             pltpu.SemaphoreType.DMA((channels,)),
             pltpu.SemaphoreType.DMA((channels,)),
-            pltpu.SemaphoreType.DMA((chunks,)),
+            pltpu.SemaphoreType.DMA((2,)),
         ],
         compiler_params=pltpu.CompilerParams(vmem_limit_bytes=57 * 2**20),
         name="columns",
@@ -305,18 +356,26 @@
         in_specs=[whole_vmem] * 2,
         out_specs=whole_vmem,
         out_shape=jax.ShapeDtypeStruct((slots, GROUP, packed), BF16),
-        scratch_shapes=[pltpu.VMEM((table.shape[1], channels * LANES), BF16)],
+        scratch_shapes=[pltpu.VMEM((table.shape[1], 2 * channels * LANES), BF16)],
         compiler_params=limit,
         name="rows",
     )(g, jnp.asarray(table))
     f = lax.all_to_all(f, "slot", 0, 0, tiled=True)
 
-    own = pl.pallas_call(
+    own, sent, pick = pl.pallas_call(
         lag_kernel,
-        in_specs=[pl.BlockSpec(memory_space=pltpu.SMEM), whole_vmem],
-        out_specs=whole_vmem,
-        out_shape=jax.ShapeDtypeStruct((entries, GROUP, packed), BF16),
-        scratch_shapes=[pltpu.VMEM((slots, GROUP, packed), F32)],
+        in_specs=[pl.BlockSpec(memory_space=pl.ANY), whole_vmem],
+        out_specs=[whole_vmem] * 3,
+        out_shape=[
+            jax.ShapeDtypeStruct((2 * entries, GROUP, packed // 2), BF16),
+            jax.ShapeDtypeStruct((2 * entries - 1, GROUP, packed // 2), BF16),
+            jax.ShapeDtypeStruct((entries, 2, GROUP, LANES), BF16),
+        ],
+        scratch_shapes=[
+            pltpu.VMEM((slots, GROUP, packed), F32),
+            pltpu.SMEM((entries,), jnp.int32),
+            pltpu.SemaphoreType.DMA(()),
+        ],
         compiler_params=limit,
         name="lags",
     )(lag_list, f)
@@ -324,18 +383,20 @@
     mirror = [
         (s * parts + p, (slots - 1 - s) * parts + parts - 1 - p) for s in range(slots) for p in range(parts)
     ]
-    other = lax.ppermute(own, ("slot", "row"), mirror)
+    other = lax.ppermute(sent, ("slot", "row"), mirror)
 
     planes = 2 * entries * channels
     return pl.pallas_call(
         functools.partial(place_kernel, half, channels, rows_up),
-        in_specs=[whole_vmem] * 3,
+        in_specs=[whole_vmem] * 4,
         out_specs=whole_vmem,
         out_shape=jax.ShapeDtypeStruct((2, entries, channels, ky_block, block), F32),
-        scratch_shapes=[pltpu.VMEM((planes * rows_up, 2 * LANES), BF16), pltpu.VMEM((rows_up, planes * LANES), BF16)],
+        scratch_shapes=[
+            pltpu.VMEM((entries, GROUP, packed // 2), BF16),
+            pltpu.VMEM((planes * rows_up, 2 * LANES), BF16), pltpu.VMEM((rows_up, planes * LANES), BF16)],
         compiler_params=limit,
         name="place",
-    )(own, other, jnp.asarray(spread_table(block, half)))
+    )(own, other, pick, jnp.asarray(spread_table(block, half)))
 
 
 def solution(mesh):

time: 82.9 us -> 81 us (0.977)
  Pallas kernels: 12 us -> 10.9 us
  waiting for transfers between devices: 15.6 us -> 14.5 us
    ppermute x1, waiting for transfers between devices: 15.6 us -> 14.5 us  [on_device(): other = lax.ppermute(sent, ('slot', 'row'), mirror)]
where the time goes in v4:
time: 81 us; the launch traced here: 80.8 us
  blocking collectives  53.9 us (67%)
  waiting for transfers between devices  14.5 us (18%)
  Pallas kernels  10.9 us (13%)
  starting transfers between devices  1.38 us (2%)
    all_to_all x1, blocking collectives, on_device(): g = lax.all_to_all(g, 'row', 0, 0, tiled=True)  32.9 us
    all_to_all x1, blocking collectives, on_device(): f = lax.all_to_all(f, 'slot', 0, 0, tiled=True)  21 us
    ppermute x1, waiting for transfers between devices, on_device(): other = lax.ppermute(sent, ('slot', 'row'), mirror)  14.5 us
    pallas_call x1, Pallas kernels, on_device(): pl.pallas_call(functools.partial(column_kernel, width, pitch), in_specs=[...  5.18 us
    pallas_call x1, Pallas kernels, on_device(): pl.pallas_call(functools.partial(row_kernel, half, channels, rows_up), in...  2.52 us
    pallas_call x1, Pallas kernels, on_device(): pl.pallas_call(functools.partial(place_kernel, half, channels, rows_up),...  1.66 us
  transfers between devices with their start and end apart: 1, of which 1 were waited for; matrix products, arithmetic and copies ran while one was open for 0% of the time, Pallas kernels for 0%

profile of v4, /device:TPU:1, one launch (start us, length us, event | category | flops | bytes accessed | tf_op | source)
XLA Modules:
  0.0 80.8 jit_solution(6478255299595886513)
XLA Ops:
  0.0 0.0 copy-start
  0.0 5.2 %columns.1 = bf16[16,16,1536]{2,1,0:T(8,128)(2,1)} custom-call(bf16[1,3,88,1408]{3,2,1,0:T(8,128)(2,1)} %x_hbm.1, s32[1,3,88,1408]{3,2,1,0:T(8,128)} %mask_hbm.1, bf16[1408,768]{1,0:T(8,128)(2,1)} %constant.6.clone.table_hbm), custom_call_target="tpu_custom_call" | custom-call | tf_op jit(solution)/shard_map/columns/pallas_call | solution.py:323
  5.2 32.9 %all_to_all.10.x_ref = bf16[16,16,1536]{2,1,0:T(8,128)(2,1)S(1)} all-to-all(bf16[16,16,1536]{2,1,0:T(8,128)(2,1)} %columns.1), channel_id=1, replica_groups=mesh['slot'=16,'row'=16] {'row'}, dimensions={0} | all-to-all | bytes 1572864 | tf_op jit(solution)/shard_map/all_to_all | solution.py:341
  38.1 0.0 copy-done
  38.1 0.0 copy-start.2
  38.1 2.5 %rows.1 = bf16[16,16,1536]{2,1,0:T(8,128)(2,1)S(1)} custom-call(bf16[16,16,1536]{2,1,0:T(8,128)(2,1)S(1)} %all_to_all.10.x_ref, bf16[768,1536]{1,0:T(8,128)(2,1)S(1)} %copy-done), custom_call_target="tpu_custom_call" | custom-call | tf_op jit(solution)/shard_map/rows/pallas_call | solution.py:354
  40.6 0.0 copy-start.1
  40.7 21.0 %all_to_all.11.z_ref = bf16[16,16,1536]{2,1,0:T(8,128)(2,1)S(1)} all-to-all(bf16[16,16,1536]{2,1,0:T(8,128)(2,1)S(1)} %rows.1), channel_id=1, replica_groups=mesh['slot'=16,'row'=16] {'slot'}, dimensions={0} | all-to-all | bytes 1572864 | tf_op jit(solution)/shard_map/all_to_all | solution.py:363
  61.7 0.0 copy-done.2
  61.7 1.6 %lags.1 = (bf16[8,16,768]{2,1,0:T(8,128)(2,1)S(1)}, bf16[7,16,768]{2,1,0:T(8,128)(2,1)S(1)}, bf16[4,2,16,128]{3,2,1,0:T(8,128)(2,1)S(1)}) custom-call(s32[4]{0:T(128)S(1)} %copy-done.2, bf16[16,16,1536]{2,1,0:T(8,128)(2,1)S(1)} %all_to_all.11.z_ref), custom_call_target="tpu_custom_call" | custom-call | tf_op jit(solution)/shard_map/lags/pallas_call | solution.py:365
  63.3 1.4 %collective-permute-start = (bf16[7,16,768]{2,1,0:T(8,128)(2,1)S(1)}, bf16[7,16,768]{2,1,0:T(8,128)(2,1)S(1)}, u32[]{:S(2)}, u32[]{:S(2)}) collective-permute-start(bf16[7,16,768]{2,1,0:T(8,128)(2,1)S(1)} %get-tuple-element.9), channel_id=1, source_target_pairs={{0,255},{1,254},{2,253},{3,252},{4,251},{5,250},{6,249},{7,248},{8... | collective-permute-start | bytes 516104 | tf_op jit(solution)/shard_map/ppermute | solution.py:386
  64.7 14.5 %collective-permute-done.other_ref = bf16[7,16,768]{2,1,0:T(8,128)(2,1)S(1)} collective-permute-done((bf16[7,16,768]{2,1,0:T(8,128)(2,1)S(1)}, bf16[7,16,768]{2,1,0:T(8,128)(2,1)S(1)}, u32[]{:S(2)}, u32[]{:S(2)}) %collective-permute-start) | collective-permute-done | bytes 172064 | tf_op jit(solution)/shard_map/ppermute | solution.py:386
  79.1 0.0 copy-done.1
  79.1 1.7 %place.1 = f32[2,4,3,88,88]{4,3,2,1,0:T(8,128)} custom-call(bf16[8,16,768]{2,1,0:T(8,128)(2,1)S(1)} %get-tuple-element.8.own_ref, bf16[7,16,768]{2,1,0:T(8,128)(2,1)S(1)} %collective-permute-done.other_ref, bf16[4,2,16,128]{3,2,1,0:T(8,128)(2,1)S(1)} %get-tuple-element.10.pick_ref, bf16[2,256,128]{2,1,0:T(8,128)(2,1)S(1)} %copy-done.1), custom_call_target="tpu_custom_call" | custom-call | tf_op jit(solution)/shard_map/place/pallas_call | solution.py:389
Async XLA Ops:
  0.0 38.1 %copy-start = (bf16[768,1536]{1,0:T(8,128)(2,1)S(1)}, bf16[768,1536]{1,0:T(8,128)(2,1)}, u32[]{:S(2)}) copy-start(bf16[768,1536]{1,0:T(8,128)(2,1)} %constant.7.clone.table_ref) | copy-start | bytes 7077892
  38.1 23.6 %copy-start.2 = (s32[4]{0:T(128)S(1)}, s32[4]{0:T(128)}, u32[]{:S(2)}) copy-start(s32[4]{0:T(128)} %lag_hbm.1) | copy-start | bytes 52
  40.6 38.5 %copy-start.1 = (bf16[2,256,128]{2,1,0:T(8,128)(2,1)S(1)}, bf16[2,256,128]{2,1,0:T(8,128)(2,1)}, u32[]{:S(2)}) copy-start(bf16[2,256,128]{2,1,0:T(8,128)(2,1)} %constant.8.clone.spread_ref) | copy-start | bytes 393220
  63.3 15.9 %collective-permute-start = (bf16[7,16,768]{2,1,0:T(8,128)(2,1)S(1)}, bf16[7,16,768]{2,1,0:T(8,128)(2,1)S(1)}, u32[]{:S(2)}, u32[]{:S(2)}) collective-permute-start(bf16[7,16,768]{2,1,0:T(8,128)(2,1)S(1)} %get-tuple-element.9), channel_id=1, source_target_pairs={{0,255},{1,254},{2,253},{3,252},{4,251},{5,250},{6,249},{7,248},{8... | collective-permute-start | bytes 516104 | tf_op jit(solution)/shard_map/ppermute | solution.py:386

commit v5 on v4

--- a/solution.py
+++ b/solution.py
@@ -230,7 +230,9 @@
             )
 
         zero = jnp.zeros((rows, middle), F32)
-        sums = lax.fori_loop(0, slots - lag, add, (zero, zero))
+        count = slots - lag
+        sums = lax.fori_loop(0, count // 2, lambda i, sums: add(2 * i + 1, add(2 * i, sums)), (zero, zero))
+        sums = lax.fori_loop(count // 2 * 2, count, add, sums)
         scale = 1.0 / jnp.broadcast_to((slots - lag).astype(F32), (rows, LANES))
         place = entries + entry - jnp.where(entry > still, 1, 0)
         for at in range(0, middle, LANES):
@@ -244,7 +246,7 @@
             sent_ref[place] = own_ref[entries + entry]
 
 
-def place_kernel(half, channels, rows_up, own_ref, other_ref, pick_ref, spread_ref, out_ref, imag, both, spread):
+def place_kernel(half, channels, rows_up, own_ref, other_ref, pick_ref, spread_ref, out_hbm, out_ref, imag, both, spread, out_sem):
     block = out_ref.shape[3]
     whole = rows_up - GROUP
     groups = channels * (rows_up // GROUP - 1) + (channels + 2) // 2
@@ -284,12 +286,21 @@
                 at = (part * entries + entry) * channels + c
                 value = jnp.dot(both[at * rows_up : (at + 1) * rows_up], spread_ref[part], preferred_element_type=F32)
                 spread[:, at * LANES : (at + 1) * LANES] = value.astype(BF16)
+    copies = []
     for part in range(2):
         for entry in range(entries):
             for c in range(channels):
                 at = (part * entries + entry) * channels + c
                 value = jnp.dot(order, spread[:, at * LANES : (at + 1) * LANES], preferred_element_type=F32)
                 out_ref[part, entry, c] = value[:block, :block]
+            copies.append(
+                pltpu.make_async_copy(
+                    out_ref.at[part, entry], out_hbm.at[part, entry], out_sem.at[part * entries + entry]
+                )
+            )
+            copies[-1].start()
+    for copy in copies:
+        copy.wait()
 
 
 def spread_table(block, half):
@@ -324,7 +335,7 @@
         functools.partial(column_kernel, width, pitch),
         in_specs=[pl.BlockSpec(memory_space=pl.ANY)] * 3,
         out_specs=whole_vmem,
-        out_shape=jax.ShapeDtypeStruct((parts, GROUP, packed), BF16),
+        out_shape=pltpu.VMEM((parts, GROUP, packed), BF16),
         scratch_shapes=[
             pltpu.VMEM(innovation.shape[1:], BF16),
             pltpu.VMEM(clear_mask.shape[1:], jnp.int32),
@@ -335,7 +346,7 @@
             pltpu.SemaphoreType.DMA((channels,)),
             pltpu.SemaphoreType.DMA((2,)),
         ],
-        compiler_params=pltpu.CompilerParams(vmem_limit_bytes=57 * 2**20),
+        compiler_params=pltpu.CompilerParams(vmem_limit_bytes=55 * 2**20),
         name="columns",
     )(innovation, clear_mask, jnp.asarray(table))
     g = lax.all_to_all(g, "row", 0, 0, tiled=True)
@@ -389,11 +400,15 @@
     return pl.pallas_call(
         functools.partial(place_kernel, half, channels, rows_up),
         in_specs=[whole_vmem] * 4,
-        out_specs=whole_vmem,
+        out_specs=pl.BlockSpec(memory_space=pl.ANY),
         out_shape=jax.ShapeDtypeStruct((2, entries, channels, ky_block, block), F32),
         scratch_shapes=[
+            pltpu.VMEM((2, entries, channels, ky_block, block), F32),
             pltpu.VMEM((entries, GROUP, packed // 2), BF16),
-            pltpu.VMEM((planes * rows_up, 2 * LANES), BF16), pltpu.VMEM((rows_up, planes * LANES), BF16)],
+            pltpu.VMEM((planes * rows_up, 2 * LANES), BF16),
+            pltpu.VMEM((rows_up, planes * LANES), BF16),
+            pltpu.SemaphoreType.DMA((2 * entries,)),
+        ],
         compiler_params=limit,
         name="place",
     )(own, other, pick, jnp.asarray(spread_table(block, half)))

time: 81 us -> 79.7 us (0.984)
  Pallas kernels: 10.9 us -> 9.86 us
    pallas_call x1, Pallas kernels: 5.18 us -> 4.29 us  [on_device(): pl.pallas_call(functools.partial(column_kernel, width, pitch), in_specs=[...]
where the time goes in v5:
time: 79.7 us; the launch traced here: 79.5 us
  blocking collectives  53.7 us (67%)
  waiting for transfers between devices  14.5 us (18%)
  Pallas kernels  9.86 us (12%)
  starting transfers between devices  1.34 us (2%)
    all_to_all x1, blocking collectives, on_device(): g = lax.all_to_all(g, 'row', 0, 0, tiled=True)  32.7 us
    all_to_all x1, blocking collectives, on_device(): f = lax.all_to_all(f, 'slot', 0, 0, tiled=True)  21 us
    ppermute x1, waiting for transfers between devices, on_device(): other = lax.ppermute(sent, ('slot', 'row'), mirror)  14.5 us
    pallas_call x1, Pallas kernels, on_device(): pl.pallas_call(functools.partial(column_kernel, width, pitch), in_specs=[...  4.29 us
    pallas_call x1, Pallas kernels, on_device(): pl.pallas_call(functools.partial(row_kernel, half, channels, rows_up), in...  2.51 us
    pallas_call x1, Pallas kernels, on_device(): pl.pallas_call(functools.partial(place_kernel, half, channels, rows_up),...  1.6 us
  transfers between devices with their start and end apart: 1, of which 1 were waited for; matrix products, arithmetic and copies ran while one was open for 0% of the time, Pallas kernels for 0%

profile of v5, /device:TPU:1, one launch (start us, length us, event | category | flops | bytes accessed | tf_op | source)
XLA Modules:
  0.0 79.5 jit_solution(12554046071599080547)
XLA Ops:
  0.0 0.0 copy-start
  0.0 4.3 %columns.1 = bf16[16,16,1536]{2,1,0:T(8,128)(2,1)S(1)} custom-call(bf16[1,3,88,1408]{3,2,1,0:T(8,128)(2,1)} %x_hbm.1, s32[1,3,88,1408]{3,2,1,0:T(8,128)} %mask_hbm.1, bf16[1408,768]{1,0:T(8,128)(2,1)} %constant.6.clone.table_hbm), custom_call_target="tpu_custom_call" | custom-call | tf_op jit(solution)/shard_map/columns/pallas_call | solution.py:334
  4.3 32.7 %all_to_all.10.x_ref = bf16[16,16,1536]{2,1,0:T(8,128)(2,1)S(1)} all-to-all(bf16[16,16,1536]{2,1,0:T(8,128)(2,1)S(1)} %columns.1), channel_id=1, replica_groups=mesh['slot'=16,'row'=16] {'row'}, dimensions={0} | all-to-all | bytes 1572864 | tf_op jit(solution)/shard_map/all_to_all | solution.py:352
  37.0 0.0 copy-done
  37.0 0.0 copy-start.2
  37.0 2.5 %rows.1 = bf16[16,16,1536]{2,1,0:T(8,128)(2,1)S(1)} custom-call(bf16[16,16,1536]{2,1,0:T(8,128)(2,1)S(1)} %all_to_all.10.x_ref, bf16[768,1536]{1,0:T(8,128)(2,1)S(1)} %copy-done), custom_call_target="tpu_custom_call" | custom-call | tf_op jit(solution)/shard_map/rows/pallas_call | solution.py:365
  39.5 0.0 copy-start.1
  39.6 21.0 %all_to_all.11.z_ref = bf16[16,16,1536]{2,1,0:T(8,128)(2,1)S(1)} all-to-all(bf16[16,16,1536]{2,1,0:T(8,128)(2,1)S(1)} %rows.1), channel_id=1, replica_groups=mesh['slot'=16,'row'=16] {'slot'}, dimensions={0} | all-to-all | bytes 1572864 | tf_op jit(solution)/shard_map/all_to_all | solution.py:374
  60.6 0.0 copy-done.2
  60.6 1.5 %lags.1 = (bf16[8,16,768]{2,1,0:T(8,128)(2,1)S(1)}, bf16[7,16,768]{2,1,0:T(8,128)(2,1)S(1)}, bf16[4,2,16,128]{3,2,1,0:T(8,128)(2,1)S(1)}) custom-call(s32[4]{0:T(128)S(1)} %copy-done.2, bf16[16,16,1536]{2,1,0:T(8,128)(2,1)S(1)} %all_to_all.11.z_ref), custom_call_target="tpu_custom_call" | custom-call | tf_op jit(solution)/shard_map/lags/pallas_call | solution.py:376
  62.1 1.3 %collective-permute-start = (bf16[7,16,768]{2,1,0:T(8,128)(2,1)S(1)}, bf16[7,16,768]{2,1,0:T(8,128)(2,1)S(1)}, u32[]{:S(2)}, u32[]{:S(2)}) collective-permute-start(bf16[7,16,768]{2,1,0:T(8,128)(2,1)S(1)} %get-tuple-element.9), channel_id=1, source_target_pairs={{0,255},{1,254},{2,253},{3,252},{4,251},{5,250},{6,249},{7,248},{8... | collective-permute-start | bytes 516104 | tf_op jit(solution)/shard_map/ppermute | solution.py:397
  63.4 14.5 %collective-permute-done.other_ref = bf16[7,16,768]{2,1,0:T(8,128)(2,1)S(1)} collective-permute-done((bf16[7,16,768]{2,1,0:T(8,128)(2,1)S(1)}, bf16[7,16,768]{2,1,0:T(8,128)(2,1)S(1)}, u32[]{:S(2)}, u32[]{:S(2)}) %collective-permute-start) | collective-permute-done | bytes 172064 | tf_op jit(solution)/shard_map/ppermute | solution.py:397
  77.9 0.0 copy-done.1
  77.9 1.6 %place.1 = f32[2,4,3,88,88]{4,3,2,1,0:T(8,128)} custom-call(bf16[8,16,768]{2,1,0:T(8,128)(2,1)S(1)} %get-tuple-element.8.own_ref, bf16[7,16,768]{2,1,0:T(8,128)(2,1)S(1)} %collective-permute-done.other_ref, bf16[4,2,16,128]{3,2,1,0:T(8,128)(2,1)S(1)} %get-tuple-element.10.pick_ref, bf16[2,256,128]{2,1,0:T(8,128)(2,1)S(1)} %copy-done.1), custom_call_target="tpu_custom_call" | custom-call | tf_op jit(solution)/shard_map/place/pallas_call | solution.py:400
Async XLA Ops:
  0.0 37.0 %copy-start = (bf16[768,1536]{1,0:T(8,128)(2,1)S(1)}, bf16[768,1536]{1,0:T(8,128)(2,1)}, u32[]{:S(2)}) copy-start(bf16[768,1536]{1,0:T(8,128)(2,1)} %constant.7.clone.table_ref) | copy-start | bytes 7077892
  37.0 23.6 %copy-start.2 = (s32[4]{0:T(128)S(1)}, s32[4]{0:T(128)}, u32[]{:S(2)}) copy-start(s32[4]{0:T(128)} %lag_hbm.1) | copy-start | bytes 52
  39.5 38.4 %copy-start.1 = (bf16[2,256,128]{2,1,0:T(8,128)(2,1)S(1)}, bf16[2,256,128]{2,1,0:T(8,128)(2,1)}, u32[]{:S(2)}) copy-start(bf16[2,256,128]{2,1,0:T(8,128)(2,1)} %constant.8.clone.spread_ref) | copy-start | bytes 393220
  62.1 15.9 %collective-permute-start = (bf16[7,16,768]{2,1,0:T(8,128)(2,1)S(1)}, bf16[7,16,768]{2,1,0:T(8,128)(2,1)S(1)}, u32[]{:S(2)}, u32[]{:S(2)}) collective-permute-start(bf16[7,16,768]{2,1,0:T(8,128)(2,1)S(1)} %get-tuple-element.9), channel_id=1, source_target_pairs={{0,255},{1,254},{2,253},{3,252},{4,251},{5,250},{6,249},{7,248},{8... | collective-permute-start | bytes 516104 | tf_op jit(solution)/shard_map/ppermute | solution.py:397

commit v6 on v5

--- a/solution.py
+++ b/solution.py
@@ -14,7 +14,6 @@
 BF16 = jnp.bfloat16
 LANES = 128
 GROUP = 16
-CUT = 768
 
 
 def phase(numbers, length):
@@ -76,42 +75,66 @@
 
 
 def column_kernel(
-    width, pitch, x_hbm, mask_hbm, table_hbm, out_ref, x, mask, table, left, result, x_sem, mask_sem, table_sem
+    width,
+    pitch,
+    x_hbm,
+    mask_hbm,
+    table_hbm,
+    next_hbm,
+    out_ref,
+    next_ref,
+    x,
+    mask,
+    table,
+    wide,
+    left,
+    result,
+    x_sem,
+    mask_sem,
+    table_sem,
+    next_sem,
 ):
     channels, rows = x.shape[0], x.shape[1]
     parts, used = out_ref.shape[0], left.shape[0] // 2
     x_copies = [pltpu.make_async_copy(x_hbm.at[0, c], x.at[c], x_sem.at[c]) for c in range(channels)]
     mask_copies = [pltpu.make_async_copy(mask_hbm.at[0, c], mask.at[c], mask_sem.at[c]) for c in range(channels)]
-    cuts = [slice(0, CUT), slice(CUT, table.shape[0])]
-    table_copies = [pltpu.make_async_copy(table_hbm.at[k], table.at[k], table_sem.at[n]) for n, k in enumerate(cuts)]
+    table_copy = pltpu.make_async_copy(table_hbm, table, table_sem)
     for c in range(channels):
         mask_copies[c].start()
         x_copies[c].start()
-    for copy in table_copies:
-        copy.start()
-    whole = rows // GROUP * GROUP
+    table_copy.start()
+    next_copy = pltpu.make_async_copy(next_hbm, next_ref, next_sem)
+    next_copy.start()
+    groups, eight = rows // GROUP, GROUP // 2
     tail = []
 
-    def store(at, value):
+    def store(group, pieces):
+        value = jnp.concatenate(pieces, axis=0)
         odd = lane_index(value.shape) % 2 == 1
-        left[at : at + value.shape[0]] = value.astype(BF16)
-        left[used + at : used + at + value.shape[0]] = jnp.where(odd, -value, value).astype(BF16)
+        at = group * GROUP
+        left[at : at + GROUP] = value.astype(BF16)
+        left[used + at : used + at + GROUP] = jnp.where(odd, -value, value).astype(BF16)
 
     for c in range(channels):
         mask_copies[c].wait()
         x_copies[c].wait()
-        masked = x[c].astype(F32) * mask[c].astype(F32)
-        store(c * whole, masked[:whole])
-        tail.append(masked[whole:])
-    spare = used - channels * rows
-    if spare:
-        tail.append(jnp.zeros((spare, left.shape[1]), F32))
-    store(channels * whole, jnp.concatenate(tail, axis=0))
-
-    for n, k in enumerate(cuts):
-        table_copies[n].wait()
-        value = jnp.dot(left[:, k], table[k], preferred_element_type=F32)
-        result[...] = result[...] + value if n else value
+        for tile in range(wide.shape[1]):
+            lanes = slice(tile * LANES, (tile + 1) * LANES)
+            wide[c, tile] = x[c, :, lanes].astype(F32) * mask[c, :, lanes].astype(F32)
+
+        def every_other(first, count):
+            return jnp.concatenate([wide[c, tile, pl.ds(first, count, 2)] for tile in range(wide.shape[1])], axis=1)
+
+        for a in range(groups):
+            store(c * groups + a, [every_other(a * GROUP + parity, eight) for parity in range(2)])
+        tail.append([every_other(groups * GROUP + parity, eight // 2) for parity in range(2)])
+    if channels % 2:
+        tail.append([jnp.zeros((eight // 2, left.shape[1]), F32)] * 2)
+    for i in range(0, len(tail), 2):
+        store(channels * groups + i // 2, [tail[i + side][parity] for parity in range(2) for side in range(2)])
+
+    table_copy.wait()
+    result[...] = jnp.dot(left[...], table[...], preferred_element_type=F32)
 
     lane = lane_index((GROUP, LANES))
     for k in range(parts // 2):
@@ -125,6 +148,7 @@
                     value = jnp.where(lane >= shift, value, result[at, (tile + 1) * LANES : (tile + 2) * LANES])
                 packed.put(turn(value, g * width - shift), g * width, width)
             out_ref[side * (parts // 2) + k] = jnp.concatenate(packed.tiles, axis=1).astype(BF16)
+    next_copy.wait()
 
 
 def split_rows(blocks, whole):
@@ -153,35 +177,43 @@
     width = 2 * half
     parts = x_ref.shape[0]
     depth = parts * GROUP
-    steps = right.shape[0] // depth
+    eight = depth // 2
+    steps = right.shape[1] // eight
     tiles = out_ref.shape[2] // LANES // 2
 
     def load(tile):
         return x_ref[:, :, tile * LANES : (tile + 1) * LANES].reshape(depth, LANES)
 
-    row_in_group = lax.broadcasted_iota(jnp.int32, (depth, LANES), 0) % GROUP
-    odd_row = row_in_group % 2 == 1
-
-    def store(a, c, value):
-        at = slice(a * depth, (a + 1) * depth)
-        right[at, c * LANES : (c + 1) * LANES] = value
-        right[at, (channels + c) * LANES : (channels + c + 1) * LANES] = jnp.where(odd_row, -value, value)
+    row_in_half = lax.broadcasted_iota(jnp.int32, (eight, LANES), 0) % (GROUP // 2)
 
     for c in range(channels):
-        for a in range(steps - 1):
-            store(a, c, unpack(load, (c * (steps - 1) + a) * width, width, depth))
-        value = unpack(load, (channels * (steps - 1) + c // 2) * width, width, depth)
-        value = jnp.where((row_in_group >= GROUP // 2) == (c % 2 == 1), value, jnp.zeros((), BF16))
-        store(steps - 1, c, value)
-
-    slots = out_ref.shape[0]
+        for a in range(steps):
+            last = a == steps - 1
+            group = channels * (steps - 1) + c // 2 if last else c * (steps - 1) + a
+            value = unpack(load, group * width, width, depth).astype(F32)
+            value = value.reshape(parts, 2, GROUP // 2, LANES)
+            for parity in range(2):
+                half_rows = value[:, parity].reshape(eight, LANES)
+                if last:
+                    half_rows = jnp.where((row_in_half >= GROUP // 4) == (c % 2 == 1), half_rows, 0.0)
+                right[parity, a * eight : (a + 1) * eight, c * LANES : (c + 1) * LANES] = half_rows.astype(BF16)
+
+    slots, depth_all = out_ref.shape[0], right.shape[1]
     for q in range(slots // 4):
-        top = 2 * q * rows_up
-        result = jnp.dot(table_ref[top : top + 2 * rows_up], right[...], preferred_element_type=F32)
+        rows_here = slice(2 * q * rows_up, 2 * (q + 1) * rows_up)
+        sums = [
+            jnp.dot(
+                table_ref[rows_here, parity * depth_all : (parity + 1) * depth_all],
+                right[parity],
+                preferred_element_type=F32,
+            )
+            for parity in range(2)
+        ]
         for shifted in range(2):
+            result = sums[0] - sums[1] if shifted else sums[0] + sums[1]
             sides = []
             for at in (0, rows_up):
-                lanes = [slice((shifted * channels + c) * LANES, (shifted * channels + c + 1) * LANES) for c in range(channels)]
+                lanes = [slice(c * LANES, (c + 1) * LANES) for c in range(channels)]
                 sides.append(split_rows([result[at : at + rows_up, l] for l in lanes], rows_up - GROUP))
             out = [Packed(tiles) for _ in range(4)]
             for g, (even, odd) in enumerate(zip(*sides)):
@@ -331,46 +363,49 @@
     packed = up(left_rows // GROUP * width, LANES)
     pitch = 96
     table = column_table(cols, parts, half, pitch)
-    g = pl.pallas_call(
+    whole = rows // GROUP
+    order = [
+        p * rows + a * GROUP + 2 * (b if a < whole else b % (GROUP // 4)) + parity
+        for parity in range(2)
+        for a in range(whole + 1)
+        for p in range(parts)
+        for b in range(GROUP // 2)
+    ]
+    ky_block = length // slots
+    rows_up = up(ky_block + 1, GROUP)
+    next_table = row_table(length, slots, rows_up, np.array(order))
+    g, next_table = pl.pallas_call(
         functools.partial(column_kernel, width, pitch),
-        in_specs=[pl.BlockSpec(memory_space=pl.ANY)] * 3,
-        out_specs=whole_vmem,
-        out_shape=pltpu.VMEM((parts, GROUP, packed), BF16),
+        in_specs=[pl.BlockSpec(memory_space=pl.ANY)] * 4,
+        out_specs=[whole_vmem] * 2,
+        out_shape=[pltpu.VMEM((parts, GROUP, packed), BF16), pltpu.VMEM(next_table.shape, BF16)],
         scratch_shapes=[
             pltpu.VMEM(innovation.shape[1:], BF16),
             pltpu.VMEM(clear_mask.shape[1:], jnp.int32),
             pltpu.VMEM(table.shape, BF16),
+            pltpu.VMEM((channels, cols // LANES, rows, LANES), F32),
             pltpu.VMEM((2 * left_rows, cols), BF16),
             pltpu.VMEM((2 * left_rows, parts // 2 * pitch), F32),
             pltpu.SemaphoreType.DMA((channels,)),
             pltpu.SemaphoreType.DMA((channels,)),
-            pltpu.SemaphoreType.DMA((2,)),
+            pltpu.SemaphoreType.DMA(()),
+            pltpu.SemaphoreType.DMA(()),
         ],
         compiler_params=pltpu.CompilerParams(vmem_limit_bytes=55 * 2**20),
         name="columns",
-    )(innovation, clear_mask, jnp.asarray(table))
+    )(innovation, clear_mask, jnp.asarray(table), jnp.asarray(next_table))
     g = lax.all_to_all(g, "row", 0, 0, tiled=True)
 
-    whole = rows // GROUP
-    order = [
-        p * rows + (a * GROUP + b if a < whole else whole * GROUP + b % (GROUP // 2))
-        for a in range(whole + 1)
-        for p in range(parts)
-        for b in range(GROUP)
-    ]
-    ky_block = length // slots
-    rows_up = up(ky_block + 1, GROUP)
-    table = row_table(length, slots, rows_up, np.array(order))
     packed = 2 * up((channels * (rows_up // GROUP - 1) + (channels + 2) // 2) * half, LANES)
     f = pl.pallas_call(
         functools.partial(row_kernel, half, channels, rows_up),
         in_specs=[whole_vmem] * 2,
         out_specs=whole_vmem,
         out_shape=jax.ShapeDtypeStruct((slots, GROUP, packed), BF16),
-        scratch_shapes=[pltpu.VMEM((table.shape[1], 2 * channels * LANES), BF16)],
+        scratch_shapes=[pltpu.VMEM((2, next_table.shape[1] // 2, channels * LANES), BF16)],
         compiler_params=limit,
         name="rows",
-    )(g, jnp.asarray(table))
+    )(g, next_table)
     f = lax.all_to_all(f, "slot", 0, 0, tiled=True)
 
     own, sent, pick = pl.pallas_call(

time: 79.7 us -> 78.9 us (0.990)
  no operation moved by 1% of the time
where the time goes in v6:
time: 78.9 us; the launch traced here: 78.7 us
  blocking collectives  53.7 us (68%)
  waiting for transfers between devices  14.5 us (18%)
  Pallas kernels  9.07 us (11%)
  starting transfers between devices  1.35 us (2%)
    all_to_all x1, blocking collectives, on_device(): g = lax.all_to_all(g, 'row', 0, 0, tiled=True)  32.7 us
    all_to_all x1, blocking collectives, on_device(): f = lax.all_to_all(f, 'slot', 0, 0, tiled=True)  21 us
    ppermute x1, waiting for transfers between devices, on_device(): other = lax.ppermute(sent, ('slot', 'row'), mirror)  14.5 us
    pallas_call x1, Pallas kernels, on_device(): pl.pallas_call(functools.partial(column_kernel, width, pitch), in_specs=[...  4.05 us
    pallas_call x1, Pallas kernels, on_device(): pl.pallas_call(functools.partial(row_kernel, half, channels, rows_up), in...  2.07 us
    pallas_call x1, Pallas kernels, on_device(): pl.pallas_call(functools.partial(place_kernel, half, channels, rows_up),...  1.6 us
  transfers between devices with their start and end apart: 1, of which 1 were waited for; matrix products, arithmetic and copies ran while one was open for 0% of the time, Pallas kernels for 0%

profile of v6, /device:TPU:1, one launch (start us, length us, event | category | flops | bytes accessed | tf_op | source)
XLA Modules:
  0.0 78.7 jit_solution(15463187967591934154)
XLA Ops:
  0.0 4.1 %columns.1 = (bf16[16,16,1536]{2,1,0:T(8,128)(2,1)S(1)}, bf16[768,1536]{1,0:T(8,128)(2,1)S(1)}) custom-call(bf16[1,3,88,1408]{3,2,1,0:T(8,128)(2,1)} %x_hbm.1, s32[1,3,88,1408]{3,2,1,0:T(8,128)} %mask_hbm.1, bf16[1408,768]{1,0:T(8,128)(2,1)} %constant.6.clone.table_hbm, bf16[768,1536]{1,0:T(8,128)(2,1)} %constant.7.clone.next_hbm), custom_call_target="tpu_custom_call" | custom-call | tf_op jit(solution)/shard_map/columns/pallas_call | solution.py:377
  4.1 32.7 %all_to_all.10.x_ref = bf16[16,16,1536]{2,1,0:T(8,128)(2,1)S(1)} all-to-all(bf16[16,16,1536]{2,1,0:T(8,128)(2,1)S(1)} %get-tuple-element.10), channel_id=1, replica_groups=mesh['slot'=16,'row'=16] {'row'}, dimensions={0} | all-to-all | bytes 1572864 | tf_op jit(solution)/shard_map/all_to_all | solution.py:397
  36.8 0.0 copy-start.1
  36.8 2.1 %rows.1 = bf16[16,16,1536]{2,1,0:T(8,128)(2,1)S(1)} custom-call(bf16[16,16,1536]{2,1,0:T(8,128)(2,1)S(1)} %all_to_all.10.x_ref, bf16[768,1536]{1,0:T(8,128)(2,1)S(1)} %get-tuple-element.11.table_ref), custom_call_target="tpu_custom_call" | custom-call | tf_op jit(solution)/shard_map/rows/pallas_call | solution.py:400
  38.9 0.0 copy-start
  38.9 21.0 %all_to_all.11.z_ref = bf16[16,16,1536]{2,1,0:T(8,128)(2,1)S(1)} all-to-all(bf16[16,16,1536]{2,1,0:T(8,128)(2,1)S(1)} %rows.1), channel_id=1, replica_groups=mesh['slot'=16,'row'=16] {'slot'}, dimensions={0} | all-to-all | bytes 1572864 | tf_op jit(solution)/shard_map/all_to_all | solution.py:409
  59.9 0.0 copy-done.1
  59.9 1.4 %lags.1 = (bf16[8,16,768]{2,1,0:T(8,128)(2,1)S(1)}, bf16[7,16,768]{2,1,0:T(8,128)(2,1)S(1)}, bf16[4,2,16,128]{3,2,1,0:T(8,128)(2,1)S(1)}) custom-call(s32[4]{0:T(128)S(1)} %copy-done.1, bf16[16,16,1536]{2,1,0:T(8,128)(2,1)S(1)} %all_to_all.11.z_ref), custom_call_target="tpu_custom_call" | custom-call | tf_op jit(solution)/shard_map/lags/pallas_call | solution.py:411
  61.3 1.3 %collective-permute-start = (bf16[7,16,768]{2,1,0:T(8,128)(2,1)S(1)}, bf16[7,16,768]{2,1,0:T(8,128)(2,1)S(1)}, u32[]{:S(2)}, u32[]{:S(2)}) collective-permute-start(bf16[7,16,768]{2,1,0:T(8,128)(2,1)S(1)} %get-tuple-element.13), channel_id=1, source_target_pairs={{0,255},{1,254},{2,253},{3,252},{4,251},{5,250},{6,249},{7,248},{8... | collective-permute-start | bytes 516104 | tf_op jit(solution)/shard_map/ppermute | solution.py:432
  62.6 14.5 %collective-permute-done.other_ref = bf16[7,16,768]{2,1,0:T(8,128)(2,1)S(1)} collective-permute-done((bf16[7,16,768]{2,1,0:T(8,128)(2,1)S(1)}, bf16[7,16,768]{2,1,0:T(8,128)(2,1)S(1)}, u32[]{:S(2)}, u32[]{:S(2)}) %collective-permute-start) | collective-permute-done | bytes 172064 | tf_op jit(solution)/shard_map/ppermute | solution.py:432
  77.1 0.0 copy-done
  77.1 1.6 %place.1 = f32[2,4,3,88,88]{4,3,2,1,0:T(8,128)} custom-call(bf16[8,16,768]{2,1,0:T(8,128)(2,1)S(1)} %get-tuple-element.12.own_ref, bf16[7,16,768]{2,1,0:T(8,128)(2,1)S(1)} %collective-permute-done.other_ref, bf16[4,2,16,128]{3,2,1,0:T(8,128)(2,1)S(1)} %get-tuple-element.14.pick_ref, bf16[2,256,128]{2,1,0:T(8,128)(2,1)S(1)} %copy-done), custom_call_target="tpu_custom_call" | custom-call | tf_op jit(solution)/shard_map/place/pallas_call | solution.py:435
Async XLA Ops:
  36.8 23.1 %copy-start.1 = (s32[4]{0:T(128)S(1)}, s32[4]{0:T(128)}, u32[]{:S(2)}) copy-start(s32[4]{0:T(128)} %lag_hbm.1) | copy-start | bytes 52
  38.9 38.3 %copy-start = (bf16[2,256,128]{2,1,0:T(8,128)(2,1)S(1)}, bf16[2,256,128]{2,1,0:T(8,128)(2,1)}, u32[]{:S(2)}) copy-start(bf16[2,256,128]{2,1,0:T(8,128)(2,1)} %constant.8.clone.spread_ref) | copy-start | bytes 393220
  61.3 15.9 %collective-permute-start = (bf16[7,16,768]{2,1,0:T(8,128)(2,1)S(1)}, bf16[7,16,768]{2,1,0:T(8,128)(2,1)S(1)}, u32[]{:S(2)}, u32[]{:S(2)}) collective-permute-start(bf16[7,16,768]{2,1,0:T(8,128)(2,1)S(1)} %get-tuple-element.13), channel_id=1, source_target_pairs={{0,255},{1,254},{2,253},{3,252},{4,251},{5,250},{6,249},{7,248},{8... | collective-permute-start | bytes 516104 | tf_op jit(solution)/shard_map/ppermute | solution.py:432

commit v7 on v6

--- a/solution.py
+++ b/solution.py
@@ -230,52 +230,71 @@
                 out_ref[at] = joined.astype(BF16)
 
 
-def zero_entry(lag_ref, entries):
+def entry_of(lag_ref, entries, lag):
     found = entries - 1
     for entry in reversed(range(entries - 1)):
-        found = jnp.where(lag_ref[entry] == 0, entry, found)
+        found = jnp.where(lag_ref[entry] == lag, entry, found)
     return found
 
 
-def lag_kernel(lag_hbm, z_ref, own_ref, sent_ref, pick_ref, wide, lag_ref, lag_sem):
+def lag_kernel(lag_hbm, z_ref, own_ref, sent_ref, pick_ref, wide, known, lag_ref, lag_sem):
     slots, rows, lanes = z_ref.shape
     middle = lanes // 2
     entries = own_ref.shape[0] // 2
     lag_copy = pltpu.make_async_copy(lag_hbm, lag_ref, lag_sem)
     lag_copy.start()
-    for t in range(slots):
-        wide[t] = z_ref[t].astype(F32)
+    for at in range(0, middle, LANES):
+        tile, other = slice(at, at + LANES), slice(middle + at, middle + at + LANES)
+        values = []
+        for t in range(slots):
+            values.append((z_ref[t, :, tile].astype(F32), z_ref[t, :, other].astype(F32)))
+            wide[t, :, tile], wide[t, :, other] = values[t]
+        total = values[0][0] * values[0][0] + values[0][1] * values[0][1]
+        for real, imag in values[1:]:
+            total = total + (real * real + imag * imag)
+        early, late = values[0], values[-1]
+        known[0, :, tile] = (total * (1.0 / slots)).astype(BF16)
+        known[1, :, tile] = (early[0] * late[0] + early[1] * late[1]).astype(BF16)
+        known[2, :, tile] = (early[1] * late[0] - early[0] * late[1]).astype(BF16)
     lag_copy.wait()
-    still = zero_entry(lag_ref, entries)
+    still, longest = entry_of(lag_ref, entries, 0), entry_of(lag_ref, entries, slots - 1)
+
+    def place(entry):
+        return entries + entry - jnp.where(entry > still, 1, 0)
+
+    own_ref[still] = known[0]
+    sent_ref[still] = known[0]
+    own_ref[entries + still] = jnp.zeros((rows, middle), BF16)
+    own_ref[longest] = known[1]
+    sent_ref[longest] = known[1]
+    own_ref[entries + longest] = known[2]
+    sent_ref[place(longest)] = known[2]
     for entry in range(entries):
         for earlier, here in enumerate((entry < still, entry > still)):
             pick_ref[entry, earlier] = jnp.broadcast_to(jnp.where(here, 1.0, 0.0), pick_ref.shape[2:]).astype(BF16)
-    for entry in range(entries):
-        lag = lag_ref[entry]
-
-        def add(t, sums):
-            early_real, early_imag = wide[t, :, :middle], wide[t, :, middle:]
-            late_real, late_imag = wide[t + lag, :, :middle], wide[t + lag, :, middle:]
-            return (
-                sums[0] + (early_real * late_real + early_imag * late_imag),
-                sums[1] + (early_imag * late_real - early_real * late_imag),
-            )
-
-        zero = jnp.zeros((rows, middle), F32)
-        count = slots - lag
-        sums = lax.fori_loop(0, count // 2, lambda i, sums: add(2 * i + 1, add(2 * i, sums)), (zero, zero))
-        sums = lax.fori_loop(count // 2 * 2, count, add, sums)
-        scale = 1.0 / jnp.broadcast_to((slots - lag).astype(F32), (rows, LANES))
-        place = entries + entry - jnp.where(entry > still, 1, 0)
-        for at in range(0, middle, LANES):
-            value = (sums[0][:, at : at + LANES] * scale).astype(BF16)
-            own_ref[entry, :, at : at + LANES] = value
-            sent_ref[entry, :, at : at + LANES] = value
-            own_ref[entries + entry, :, at : at + LANES] = (sums[1][:, at : at + LANES] * scale).astype(BF16)
-
-        @pl.when(entry != still)
+
+        @pl.when((entry != still) & (entry != longest))
         def _():
-            sent_ref[place] = own_ref[entries + entry]
+            lag = lag_ref[entry]
+
+            def add(t, sums):
+                early_real, early_imag = wide[t, :, :middle], wide[t, :, middle:]
+                late_real, late_imag = wide[t + lag, :, :middle], wide[t + lag, :, middle:]
+                return (
+                    sums[0] + (early_real * late_real + early_imag * late_imag),
+                    sums[1] + (early_imag * late_real - early_real * late_imag),
+                )
+
+            zero = jnp.zeros((rows, middle), F32)
+            count = slots - lag
+            sums = lax.fori_loop(0, count // 2, lambda i, sums: add(2 * i + 1, add(2 * i, sums)), (zero, zero))
+            sums = lax.fori_loop(count // 2 * 2, count, add, sums)
+            scale = 1.0 / jnp.broadcast_to(count.astype(F32), (rows, LANES))
+            for at in range(0, middle, LANES):
+                tile = slice(at, at + LANES)
+                real, imag = [(value[:, tile] * scale).astype(BF16) for value in sums]
+                own_ref[entry, :, tile], own_ref[entries + entry, :, tile] = real, imag
+                sent_ref[entry, :, tile], sent_ref[place(entry), :, tile] = real, imag
 
 
 def place_kernel(half, channels, rows_up, own_ref, other_ref, pick_ref, spread_ref, out_hbm, out_ref, imag, both, spread, out_sem):
@@ -419,6 +438,7 @@
         ],
         scratch_shapes=[
             pltpu.VMEM((slots, GROUP, packed), F32),
+            pltpu.VMEM((3, GROUP, packed // 2), BF16),
             pltpu.SMEM((entries,), jnp.int32),
             pltpu.SemaphoreType.DMA(()),
         ],

time: 78.9 us -> 78.6 us (level)
  no operation moved by 1% of the time
where the time goes in v7:
time: 78.6 us; the launch traced here: 78.4 us
  blocking collectives  53.7 us (68%)
  waiting for transfers between devices  14.5 us (18%)
  Pallas kernels  8.77 us (11%)
  starting transfers between devices  1.35 us (2%)
    all_to_all x1, blocking collectives, on_device(): g = lax.all_to_all(g, 'row', 0, 0, tiled=True)  32.7 us
    all_to_all x1, blocking collectives, on_device(): f = lax.all_to_all(f, 'slot', 0, 0, tiled=True)  21 us
    ppermute x1, waiting for transfers between devices, on_device(): other = lax.ppermute(sent, ('slot', 'row'), mirror)  14.5 us
    pallas_call x1, Pallas kernels, on_device(): pl.pallas_call(functools.partial(column_kernel, width, pitch), in_specs=[...  4.05 us
    pallas_call x1, Pallas kernels, on_device(): pl.pallas_call(functools.partial(row_kernel, half, channels, rows_up), in...  2.07 us
    pallas_call x1, Pallas kernels, on_device(): pl.pallas_call(functools.partial(place_kernel, half, channels, rows_up),...  1.6 us
  transfers between devices with their start and end apart: 1, of which 1 were waited for; matrix products, arithmetic and copies ran while one was open for 0% of the time, Pallas kernels for 0%

profile of v7, /device:TPU:1, one launch (start us, length us, event | category | flops | bytes accessed | tf_op | source)
XLA Modules:
  0.0 78.4 jit_solution(8132945277426577354)
XLA Ops:
  0.0 4.1 %columns.1 = (bf16[16,16,1536]{2,1,0:T(8,128)(2,1)S(1)}, bf16[768,1536]{1,0:T(8,128)(2,1)S(1)}) custom-call(bf16[1,3,88,1408]{3,2,1,0:T(8,128)(2,1)} %x_hbm.1, s32[1,3,88,1408]{3,2,1,0:T(8,128)} %mask_hbm.1, bf16[1408,768]{1,0:T(8,128)(2,1)} %constant.6.clone.table_hbm, bf16[768,1536]{1,0:T(8,128)(2,1)} %constant.7.clone.next_hbm), custom_call_target="tpu_custom_call" | custom-call | tf_op jit(solution)/shard_map/columns/pallas_call | solution.py:396
  4.1 32.7 %all_to_all.10.x_ref = bf16[16,16,1536]{2,1,0:T(8,128)(2,1)S(1)} all-to-all(bf16[16,16,1536]{2,1,0:T(8,128)(2,1)S(1)} %get-tuple-element.10), channel_id=1, replica_groups=mesh['slot'=16,'row'=16] {'row'}, dimensions={0} | all-to-all | bytes 1572864 | tf_op jit(solution)/shard_map/all_to_all | solution.py:416
  36.8 0.0 copy-start.1
  36.8 2.1 %rows.1 = bf16[16,16,1536]{2,1,0:T(8,128)(2,1)S(1)} custom-call(bf16[16,16,1536]{2,1,0:T(8,128)(2,1)S(1)} %all_to_all.10.x_ref, bf16[768,1536]{1,0:T(8,128)(2,1)S(1)} %get-tuple-element.11.table_ref), custom_call_target="tpu_custom_call" | custom-call | tf_op jit(solution)/shard_map/rows/pallas_call | solution.py:419
  38.9 0.0 copy-start
  38.9 21.0 %all_to_all.11.z_ref = bf16[16,16,1536]{2,1,0:T(8,128)(2,1)S(1)} all-to-all(bf16[16,16,1536]{2,1,0:T(8,128)(2,1)S(1)} %rows.1), channel_id=1, replica_groups=mesh['slot'=16,'row'=16] {'slot'}, dimensions={0} | all-to-all | bytes 1572864 | tf_op jit(solution)/shard_map/all_to_all | solution.py:428
  59.9 0.0 copy-done.1
  59.9 1.1 %lags.1 = (bf16[8,16,768]{2,1,0:T(8,128)(2,1)S(1)}, bf16[7,16,768]{2,1,0:T(8,128)(2,1)S(1)}, bf16[4,2,16,128]{3,2,1,0:T(8,128)(2,1)S(1)}) custom-call(s32[4]{0:T(128)S(1)} %copy-done.1, bf16[16,16,1536]{2,1,0:T(8,128)(2,1)S(1)} %all_to_all.11.z_ref), custom_call_target="tpu_custom_call" | custom-call | tf_op jit(solution)/shard_map/lags/pallas_call | solution.py:430
  61.0 1.3 %collective-permute-start = (bf16[7,16,768]{2,1,0:T(8,128)(2,1)S(1)}, bf16[7,16,768]{2,1,0:T(8,128)(2,1)S(1)}, u32[]{:S(2)}, u32[]{:S(2)}) collective-permute-start(bf16[7,16,768]{2,1,0:T(8,128)(2,1)S(1)} %get-tuple-element.13), channel_id=1, source_target_pairs={{0,255},{1,254},{2,253},{3,252},{4,251},{5,250},{6,249},{7,248},{8... | collective-permute-start | bytes 516104 | tf_op jit(solution)/shard_map/ppermute | solution.py:452
  62.3 14.5 %collective-permute-done.other_ref = bf16[7,16,768]{2,1,0:T(8,128)(2,1)S(1)} collective-permute-done((bf16[7,16,768]{2,1,0:T(8,128)(2,1)S(1)}, bf16[7,16,768]{2,1,0:T(8,128)(2,1)S(1)}, u32[]{:S(2)}, u32[]{:S(2)}) %collective-permute-start) | collective-permute-done | bytes 172064 | tf_op jit(solution)/shard_map/ppermute | solution.py:452
  76.8 0.0 copy-done
  76.8 1.6 %place.1 = f32[2,4,3,88,88]{4,3,2,1,0:T(8,128)} custom-call(bf16[8,16,768]{2,1,0:T(8,128)(2,1)S(1)} %get-tuple-element.12.own_ref, bf16[7,16,768]{2,1,0:T(8,128)(2,1)S(1)} %collective-permute-done.other_ref, bf16[4,2,16,128]{3,2,1,0:T(8,128)(2,1)S(1)} %get-tuple-element.14.pick_ref, bf16[2,256,128]{2,1,0:T(8,128)(2,1)S(1)} %copy-done), custom_call_target="tpu_custom_call" | custom-call | tf_op jit(solution)/shard_map/place/pallas_call | solution.py:455
Async XLA Ops:
  36.8 23.1 %copy-start.1 = (s32[4]{0:T(128)S(1)}, s32[4]{0:T(128)}, u32[]{:S(2)}) copy-start(s32[4]{0:T(128)} %lag_hbm.1) | copy-start | bytes 52
  38.9 38.0 %copy-start = (bf16[2,256,128]{2,1,0:T(8,128)(2,1)S(1)}, bf16[2,256,128]{2,1,0:T(8,128)(2,1)}, u32[]{:S(2)}) copy-start(bf16[2,256,128]{2,1,0:T(8,128)(2,1)} %constant.8.clone.spread_ref) | copy-start | bytes 393220
  61.0 15.9 %collective-permute-start = (bf16[7,16,768]{2,1,0:T(8,128)(2,1)S(1)}, bf16[7,16,768]{2,1,0:T(8,128)(2,1)S(1)}, u32[]{:S(2)}, u32[]{:S(2)}) collective-permute-start(bf16[7,16,768]{2,1,0:T(8,128)(2,1)S(1)} %get-tuple-element.13), channel_id=1, source_target_pairs={{0,255},{1,254},{2,253},{3,252},{4,251},{5,250},{6,249},{7,248},{8... | collective-permute-start | bytes 516104 | tf_op jit(solution)/shard_map/ppermute | solution.py:452

commit v8 on v7

--- a/solution.py
+++ b/solution.py
@@ -27,7 +27,11 @@
     table = np.zeros((length, parts // 2, pitch))
     table[:, :, :half] = np.cos(angles)
     table[:, :, half : 2 * half] = -np.sin(angles)
-    return (table / math.sqrt(length)).reshape(length, parts // 2 * pitch).astype(ml_dtypes.bfloat16)
+    table = (table / math.sqrt(length)).reshape(length, parts // 2 * pitch)
+    split = np.zeros((2, up(length, 2 * LANES) // 2, parts // 2 * pitch))
+    for parity in range(2):
+        split[parity, : length // 2] = table[parity::2]
+    return split.astype(ml_dtypes.bfloat16)
 
 
 def row_table(length, parts, rows_up, row_order):
@@ -88,6 +92,8 @@
     table,
     wide,
     left,
+    halves,
+    split,
     result,
     x_sem,
     mask_sem,
@@ -95,7 +101,7 @@
     next_sem,
 ):
     channels, rows = x.shape[0], x.shape[1]
-    parts, used = out_ref.shape[0], left.shape[0] // 2
+    parts, used, cols = out_ref.shape[0], left.shape[0], x.shape[2]
     x_copies = [pltpu.make_async_copy(x_hbm.at[0, c], x.at[c], x_sem.at[c]) for c in range(channels)]
     mask_copies = [pltpu.make_async_copy(mask_hbm.at[0, c], mask.at[c], mask_sem.at[c]) for c in range(channels)]
     table_copy = pltpu.make_async_copy(table_hbm, table, table_sem)
@@ -105,15 +111,20 @@
     table_copy.start()
     next_copy = pltpu.make_async_copy(next_hbm, next_ref, next_sem)
     next_copy.start()
+    square = (2 * LANES, 2 * LANES)
+    target = lane_index(square)
+    source = target % LANES * 2 + target // LANES
+    split[...] = (lax.broadcasted_iota(jnp.int32, square, 0) == source).astype(F32).astype(BF16)
     groups, eight = rows // GROUP, GROUP // 2
     tail = []
 
     def store(group, pieces):
         value = jnp.concatenate(pieces, axis=0)
-        odd = lane_index(value.shape) % 2 == 1
         at = group * GROUP
-        left[at : at + GROUP] = value.astype(BF16)
-        left[used + at : used + at + GROUP] = jnp.where(odd, -value, value).astype(BF16)
+        left[at : at + GROUP, :cols] = value.astype(BF16)
+
+    if left.shape[1] > cols:
+        left[:, cols:] = jnp.zeros((used, left.shape[1] - cols), BF16)
 
     for c in range(channels):
         mask_copies[c].wait()
@@ -129,12 +140,19 @@
             store(c * groups + a, [every_other(a * GROUP + parity, eight) for parity in range(2)])
         tail.append([every_other(groups * GROUP + parity, eight // 2) for parity in range(2)])
     if channels % 2:
-        tail.append([jnp.zeros((eight // 2, left.shape[1]), F32)] * 2)
+        tail.append([jnp.zeros((eight // 2, cols), F32)] * 2)
     for i in range(0, len(tail), 2):
         store(channels * groups + i // 2, [tail[i + side][parity] for parity in range(2) for side in range(2)])
 
+    for tile in range(left.shape[1] // (2 * LANES)):
+        value = left[:, 2 * tile * LANES : 2 * (tile + 1) * LANES]
+        value = jnp.dot(value, split[...], preferred_element_type=F32).astype(BF16)
+        for parity in range(2):
+            halves[parity, :, tile * LANES : (tile + 1) * LANES] = value[:, parity * LANES : (parity + 1) * LANES]
     table_copy.wait()
-    result[...] = jnp.dot(left[...], table[...], preferred_element_type=F32)
+    even, odd = [jnp.dot(halves[parity], table[parity], preferred_element_type=F32) for parity in range(2)]
+    result[:used] = even + odd
+    result[used:] = even - odd
 
     lane = lane_index((GROUP, LANES))
     for k in range(parts // 2):
@@ -403,7 +421,9 @@
             pltpu.VMEM(clear_mask.shape[1:], jnp.int32),
             pltpu.VMEM(table.shape, BF16),
             pltpu.VMEM((channels, cols // LANES, rows, LANES), F32),
-            pltpu.VMEM((2 * left_rows, cols), BF16),
+            pltpu.VMEM((left_rows, up(cols, 2 * LANES)), BF16),
+            pltpu.VMEM((2, left_rows, up(cols, 2 * LANES) // 2), BF16),
+            pltpu.VMEM((2 * LANES, 2 * LANES), BF16),
             pltpu.VMEM((2 * left_rows, parts // 2 * pitch), F32),
             pltpu.SemaphoreType.DMA((channels,)),
             pltpu.SemaphoreType.DMA((channels,)),

time: 78.6 us -> 77.9 us (level)
  no operation moved by 1% of the time
where the time goes in v8:
time: 77.9 us; the launch traced here: 77.8 us
  blocking collectives  53.6 us (69%)
  waiting for transfers between devices  14.5 us (19%)
  Pallas kernels  8.24 us (11%)
  starting transfers between devices  1.35 us (2%)
    all_to_all x1, blocking collectives, on_device(): g = lax.all_to_all(g, 'row', 0, 0, tiled=True)  32.7 us
    all_to_all x1, blocking collectives, on_device(): f = lax.all_to_all(f, 'slot', 0, 0, tiled=True)  20.9 us
    ppermute x1, waiting for transfers between devices, on_device(): other = lax.ppermute(sent, ('slot', 'row'), mirror)  14.5 us
    pallas_call x1, Pallas kernels, on_device(): pl.pallas_call(functools.partial(column_kernel, width, pitch), in_specs=[...  3.56 us
    pallas_call x1, Pallas kernels, on_device(): pl.pallas_call(functools.partial(row_kernel, half, channels, rows_up), in...  2.07 us
    pallas_call x1, Pallas kernels, on_device(): pl.pallas_call(functools.partial(place_kernel, half, channels, rows_up),...  1.59 us
  transfers between devices with their start and end apart: 1, of which 1 were waited for; matrix products, arithmetic and copies ran while one was open for 0% of the time, Pallas kernels for 0%

profile of v8, /device:TPU:1, one launch (start us, length us, event | category | flops | bytes accessed | tf_op | source)
XLA Modules:
  0.0 77.8 jit_solution(16993806843126868687)
XLA Ops:
  0.0 3.6 %columns.1 = (bf16[16,16,1536]{2,1,0:T(8,128)(2,1)S(1)}, bf16[768,1536]{1,0:T(8,128)(2,1)S(1)}) custom-call(bf16[1,3,88,1408]{3,2,1,0:T(8,128)(2,1)} %x_hbm.1, s32[1,3,88,1408]{3,2,1,0:T(8,128)} %mask_hbm.1, bf16[2,768,768]{2,1,0:T(8,128)(2,1)} %constant.6.clone.table_hbm, bf16[768,1536]{1,0:T(8,128)(2,1)} %constant.7.clone.next_hbm), custom_call_target="tpu_custom_call" | custom-call | tf_op jit(solution)/shard_map/columns/pallas_call | solution.py:414
  3.6 32.7 %all_to_all.10.x_ref = bf16[16,16,1536]{2,1,0:T(8,128)(2,1)S(1)} all-to-all(bf16[16,16,1536]{2,1,0:T(8,128)(2,1)S(1)} %get-tuple-element.10), channel_id=1, replica_groups=mesh['slot'=16,'row'=16] {'row'}, dimensions={0} | all-to-all | bytes 1572864 | tf_op jit(solution)/shard_map/all_to_all | solution.py:436
  36.3 0.0 copy-start.1
  36.3 0.0 copy-start
  36.3 2.1 %rows.1 = bf16[16,16,1536]{2,1,0:T(8,128)(2,1)S(1)} custom-call(bf16[16,16,1536]{2,1,0:T(8,128)(2,1)S(1)} %all_to_all.10.x_ref, bf16[768,1536]{1,0:T(8,128)(2,1)S(1)} %get-tuple-element.11.table_ref), custom_call_target="tpu_custom_call" | custom-call | tf_op jit(solution)/shard_map/rows/pallas_call | solution.py:439
  38.4 20.9 %all_to_all.11.z_ref = bf16[16,16,1536]{2,1,0:T(8,128)(2,1)S(1)} all-to-all(bf16[16,16,1536]{2,1,0:T(8,128)(2,1)S(1)} %rows.1), channel_id=1, replica_groups=mesh['slot'=16,'row'=16] {'slot'}, dimensions={0} | all-to-all | bytes 1572864 | tf_op jit(solution)/shard_map/all_to_all | solution.py:448
  59.3 0.0 copy-done.1
  59.3 1.0 %lags.1 = (bf16[8,16,768]{2,1,0:T(8,128)(2,1)S(1)}, bf16[7,16,768]{2,1,0:T(8,128)(2,1)S(1)}, bf16[4,2,16,128]{3,2,1,0:T(8,128)(2,1)S(1)}) custom-call(s32[4]{0:T(128)S(1)} %copy-done.1, bf16[16,16,1536]{2,1,0:T(8,128)(2,1)S(1)} %all_to_all.11.z_ref), custom_call_target="tpu_custom_call" | custom-call | tf_op jit(solution)/shard_map/lags/pallas_call | solution.py:450
  60.3 1.3 %collective-permute-start = (bf16[7,16,768]{2,1,0:T(8,128)(2,1)S(1)}, bf16[7,16,768]{2,1,0:T(8,128)(2,1)S(1)}, u32[]{:S(2)}, u32[]{:S(2)}) collective-permute-start(bf16[7,16,768]{2,1,0:T(8,128)(2,1)S(1)} %get-tuple-element.13), channel_id=1, source_target_pairs={{0,255},{1,254},{2,253},{3,252},{4,251},{5,250},{6,249},{7,248},{8... | collective-permute-start | bytes 516104 | tf_op jit(solution)/shard_map/ppermute | solution.py:472
  61.6 14.5 %collective-permute-done.other_ref = bf16[7,16,768]{2,1,0:T(8,128)(2,1)S(1)} collective-permute-done((bf16[7,16,768]{2,1,0:T(8,128)(2,1)S(1)}, bf16[7,16,768]{2,1,0:T(8,128)(2,1)S(1)}, u32[]{:S(2)}, u32[]{:S(2)}) %collective-permute-start) | collective-permute-done | bytes 172064 | tf_op jit(solution)/shard_map/ppermute | solution.py:472
  76.2 0.0 copy-done
  76.2 1.6 %place.1 = f32[2,4,3,88,88]{4,3,2,1,0:T(8,128)} custom-call(bf16[8,16,768]{2,1,0:T(8,128)(2,1)S(1)} %get-tuple-element.12.own_ref, bf16[7,16,768]{2,1,0:T(8,128)(2,1)S(1)} %collective-permute-done.other_ref, bf16[4,2,16,128]{3,2,1,0:T(8,128)(2,1)S(1)} %get-tuple-element.14.pick_ref, bf16[2,256,128]{2,1,0:T(8,128)(2,1)S(1)} %copy-done), custom_call_target="tpu_custom_call" | custom-call | tf_op jit(solution)/shard_map/place/pallas_call | solution.py:475
Async XLA Ops:
  36.3 23.0 %copy-start.1 = (s32[4]{0:T(128)S(1)}, s32[4]{0:T(128)}, u32[]{:S(2)}) copy-start(s32[4]{0:T(128)} %lag_hbm.1) | copy-start | bytes 52
  36.3 39.9 %copy-start = (bf16[2,256,128]{2,1,0:T(8,128)(2,1)S(1)}, bf16[2,256,128]{2,1,0:T(8,128)(2,1)}, u32[]{:S(2)}) copy-start(bf16[2,256,128]{2,1,0:T(8,128)(2,1)} %constant.8.clone.spread_ref) | copy-start | bytes 393220
  60.3 15.9 %collective-permute-start = (bf16[7,16,768]{2,1,0:T(8,128)(2,1)S(1)}, bf16[7,16,768]{2,1,0:T(8,128)(2,1)S(1)}, u32[]{:S(2)}, u32[]{:S(2)}) collective-permute-start(bf16[7,16,768]{2,1,0:T(8,128)(2,1)S(1)} %get-tuple-element.13), channel_id=1, source_target_pairs={{0,255},{1,254},{2,253},{3,252},{4,251},{5,250},{6,249},{7,248},{8... | collective-permute-start | bytes 516104 | tf_op jit(solution)/shard_map/ppermute | solution.py:472

commit v9 on v8

--- a/solution.py
+++ b/solution.py
@@ -28,10 +28,7 @@
     table[:, :, :half] = np.cos(angles)
     table[:, :, half : 2 * half] = -np.sin(angles)
     table = (table / math.sqrt(length)).reshape(length, parts // 2 * pitch)
-    split = np.zeros((2, up(length, 2 * LANES) // 2, parts // 2 * pitch))
-    for parity in range(2):
-        split[parity, : length // 2] = table[parity::2]
-    return split.astype(ml_dtypes.bfloat16)
+    return np.stack([table[parity::2] for parity in range(2)]).astype(ml_dtypes.bfloat16)
 
 
 def row_table(length, parts, rows_up, row_order):
@@ -104,13 +101,16 @@
     parts, used, cols = out_ref.shape[0], left.shape[0], x.shape[2]
     x_copies = [pltpu.make_async_copy(x_hbm.at[0, c], x.at[c], x_sem.at[c]) for c in range(channels)]
     mask_copies = [pltpu.make_async_copy(mask_hbm.at[0, c], mask.at[c], mask_sem.at[c]) for c in range(channels)]
-    table_copy = pltpu.make_async_copy(table_hbm, table, table_sem)
+    filled = table_hbm.shape[1]
+    table_copy = pltpu.make_async_copy(table_hbm, table.at[:, :filled], table_sem)
     for c in range(channels):
         mask_copies[c].start()
         x_copies[c].start()
     table_copy.start()
     next_copy = pltpu.make_async_copy(next_hbm, next_ref, next_sem)
     next_copy.start()
+    if filled < table.shape[1]:
+        table[:, filled:] = jnp.zeros((2, table.shape[1] - filled, table.shape[2]), BF16)
     square = (2 * LANES, 2 * LANES)
     target = lane_index(square)
     source = target % LANES * 2 + target // LANES
@@ -419,7 +419,7 @@
         scratch_shapes=[
             pltpu.VMEM(innovation.shape[1:], BF16),
             pltpu.VMEM(clear_mask.shape[1:], jnp.int32),
-            pltpu.VMEM(table.shape, BF16),
+            pltpu.VMEM((2, up(cols, 2 * LANES) // 2, table.shape[2]), BF16),
             pltpu.VMEM((channels, cols // LANES, rows, LANES), F32),
             pltpu.VMEM((left_rows, up(cols, 2 * LANES)), BF16),
             pltpu.VMEM((2, left_rows, up(cols, 2 * LANES) // 2), BF16),

time: 77.9 us -> 78.3 us (level)
  no operation moved by 1% of the time
where the time goes in v9:
time: 78.3 us; the launch traced here: 78.2 us
  blocking collectives  53.7 us (69%)
  waiting for transfers between devices  14.5 us (19%)
  Pallas kernels  8.53 us (11%)
  starting transfers between devices  1.36 us (2%)
    all_to_all x1, blocking collectives, on_device(): g = lax.all_to_all(g, 'row', 0, 0, tiled=True)  32.7 us
    all_to_all x1, blocking collectives, on_device(): f = lax.all_to_all(f, 'slot', 0, 0, tiled=True)  21 us
    ppermute x1, waiting for transfers between devices, on_device(): other = lax.ppermute(sent, ('slot', 'row'), mirror)  14.5 us
    pallas_call x1, Pallas kernels, on_device(): pl.pallas_call(functools.partial(column_kernel, width, pitch), in_specs=[...  3.8 us
    pallas_call x1, Pallas kernels, on_device(): pl.pallas_call(functools.partial(row_kernel, half, channels, rows_up), in...  2.07 us
    pallas_call x1, Pallas kernels, on_device(): pl.pallas_call(functools.partial(place_kernel, half, channels, rows_up),...  1.59 us
  transfers between devices with their start and end apart: 1, of which 1 were waited for; matrix products, arithmetic and copies ran while one was open for 0% of the time, Pallas kernels for 0%

profile of v9, /device:TPU:1, one launch (start us, length us, event | category | flops | bytes accessed | tf_op | source)
XLA Modules:
  0.0 78.2 jit_solution(16928364975900088917)
XLA Ops:
  0.0 3.8 %columns.1 = (bf16[16,16,1536]{2,1,0:T(8,128)(2,1)S(1)}, bf16[768,1536]{1,0:T(8,128)(2,1)S(1)}) custom-call(bf16[1,3,88,1408]{3,2,1,0:T(8,128)(2,1)} %x_hbm.1, s32[1,3,88,1408]{3,2,1,0:T(8,128)} %mask_hbm.1, bf16[2,704,768]{2,1,0:T(8,128)(2,1)} %constant.6.clone.table_hbm, bf16[768,1536]{1,0:T(8,128)(2,1)} %constant.7.clone.next_hbm), custom_call_target="tpu_custom_call" | custom-call | tf_op jit(solution)/shard_map/columns/pallas_call | solution.py:414
  3.8 32.7 %all_to_all.10.x_ref = bf16[16,16,1536]{2,1,0:T(8,128)(2,1)S(1)} all-to-all(bf16[16,16,1536]{2,1,0:T(8,128)(2,1)S(1)} %get-tuple-element.10), channel_id=1, replica_groups=mesh['slot'=16,'row'=16] {'row'}, dimensions={0} | all-to-all | bytes 1572864 | tf_op jit(solution)/shard_map/all_to_all | solution.py:436
  36.5 0.0 copy-start.1
  36.5 2.1 %rows.1 = bf16[16,16,1536]{2,1,0:T(8,128)(2,1)S(1)} custom-call(bf16[16,16,1536]{2,1,0:T(8,128)(2,1)S(1)} %all_to_all.10.x_ref, bf16[768,1536]{1,0:T(8,128)(2,1)S(1)} %get-tuple-element.11.table_ref), custom_call_target="tpu_custom_call" | custom-call | tf_op jit(solution)/shard_map/rows/pallas_call | solution.py:439
  38.6 0.0 copy-start
  38.6 21.0 %all_to_all.11.z_ref = bf16[16,16,1536]{2,1,0:T(8,128)(2,1)S(1)} all-to-all(bf16[16,16,1536]{2,1,0:T(8,128)(2,1)S(1)} %rows.1), channel_id=1, replica_groups=mesh['slot'=16,'row'=16] {'slot'}, dimensions={0} | all-to-all | bytes 1572864 | tf_op jit(solution)/shard_map/all_to_all | solution.py:448
  59.6 0.0 copy-done.1
  59.6 1.1 %lags.1 = (bf16[8,16,768]{2,1,0:T(8,128)(2,1)S(1)}, bf16[7,16,768]{2,1,0:T(8,128)(2,1)S(1)}, bf16[4,2,16,128]{3,2,1,0:T(8,128)(2,1)S(1)}) custom-call(s32[4]{0:T(128)S(1)} %copy-done.1, bf16[16,16,1536]{2,1,0:T(8,128)(2,1)S(1)} %all_to_all.11.z_ref), custom_call_target="tpu_custom_call" | custom-call | tf_op jit(solution)/shard_map/lags/pallas_call | solution.py:450
  60.7 1.4 %collective-permute-start = (bf16[7,16,768]{2,1,0:T(8,128)(2,1)S(1)}, bf16[7,16,768]{2,1,0:T(8,128)(2,1)S(1)}, u32[]{:S(2)}, u32[]{:S(2)}) collective-permute-start(bf16[7,16,768]{2,1,0:T(8,128)(2,1)S(1)} %get-tuple-element.13), channel_id=1, source_target_pairs={{0,255},{1,254},{2,253},{3,252},{4,251},{5,250},{6,249},{7,248},{8... | collective-permute-start | bytes 516104 | tf_op jit(solution)/shard_map/ppermute | solution.py:472
  62.1 14.5 %collective-permute-done.other_ref = bf16[7,16,768]{2,1,0:T(8,128)(2,1)S(1)} collective-permute-done((bf16[7,16,768]{2,1,0:T(8,128)(2,1)S(1)}, bf16[7,16,768]{2,1,0:T(8,128)(2,1)S(1)}, u32[]{:S(2)}, u32[]{:S(2)}) %collective-permute-start) | collective-permute-done | bytes 172064 | tf_op jit(solution)/shard_map/ppermute | solution.py:472
  76.6 0.0 copy-done
  76.6 1.6 %place.1 = f32[2,4,3,88,88]{4,3,2,1,0:T(8,128)} custom-call(bf16[8,16,768]{2,1,0:T(8,128)(2,1)S(1)} %get-tuple-element.12.own_ref, bf16[7,16,768]{2,1,0:T(8,128)(2,1)S(1)} %collective-permute-done.other_ref, bf16[4,2,16,128]{3,2,1,0:T(8,128)(2,1)S(1)} %get-tuple-element.14.pick_ref, bf16[2,256,128]{2,1,0:T(8,128)(2,1)S(1)} %copy-done), custom_call_target="tpu_custom_call" | custom-call | tf_op jit(solution)/shard_map/place/pallas_call | solution.py:475
Async XLA Ops:
  36.5 23.1 %copy-start.1 = (s32[4]{0:T(128)S(1)}, s32[4]{0:T(128)}, u32[]{:S(2)}) copy-start(s32[4]{0:T(128)} %lag_hbm.1) | copy-start | bytes 52
  38.6 38.0 %copy-start = (bf16[2,256,128]{2,1,0:T(8,128)(2,1)S(1)}, bf16[2,256,128]{2,1,0:T(8,128)(2,1)}, u32[]{:S(2)}) copy-start(bf16[2,256,128]{2,1,0:T(8,128)(2,1)} %constant.8.clone.spread_ref) | copy-start | bytes 393220
  60.7 15.9 %collective-permute-start = (bf16[7,16,768]{2,1,0:T(8,128)(2,1)S(1)}, bf16[7,16,768]{2,1,0:T(8,128)(2,1)S(1)}, u32[]{:S(2)}, u32[]{:S(2)}) collective-permute-start(bf16[7,16,768]{2,1,0:T(8,128)(2,1)S(1)} %get-tuple-element.13), channel_id=1, source_target_pairs={{0,255},{1,254},{2,253},{3,252},{4,251},{5,250},{6,249},{7,248},{8... | collective-permute-start | bytes 516104 | tf_op jit(solution)/shard_map/ppermute | solution.py:472
